TPU v7x, 128 devices: a whole 4x4x4 slice. The times are simulated.
128 devices in a mesh: dom: 128 (over z, y, x, core).
Axes of the slice: x: 4, y: 4, z: 4, core: 2. Of those that a mesh axis runs over, the one named last changes fastest.
Arguments:
- positions: float32 [3, 65536, 128], P(None, 'dom'), may hold values from 0 to 1
- velocities: float32 [3, 65536, 128], P(None, 'dom'), may hold values from -3 to 3
- masses: float32 [65536, 128], P('dom'), may hold values from 4.8828126e-05 to 0.00048828125
- active_leaves: int32 [2048], P('dom'), may hold values from 0 to 511, as said below
- active_count: int32 [128], P('dom'), may hold values from 4 to 16, as said below
- partner_owner: int32 [2048, 16], P('dom'), may hold values from 0 to 127, as said below
- partner_leaf: int32 [2048, 16], P('dom'), may hold values from 0 to 511, as said below
- mig_leaf: int32 [2048], P('dom'), may hold values from -1 to 511
Outputs:
- new_positions: float32 [3, 65536, 128], P(None, 'dom')
- new_velocities: float32 [3, 65536, 128], P(None, 'dom')
- arrived: float32 [7, 2048, 128], P(None, 'dom')
Inputs may be any that keep to these rules, and one draw needn't show every extreme that they name: `active_leaves`: within one domain's 16 slots the leaf numbers are distinct. `active_count`: at most 16; some domain has exactly 16. `partner_owner`: the owner lies within 2 domains of the list's own domain, counted cyclically along the curve. `partner_leaf`: for each domain and each other domain within reach, its lists name exactly 8 distinct leaves of that domain. `mig_leaf`: -1 marks an empty slot.
All inputs are finite; a program needn't handle non-finite values.
Results may differ from a plain program's by a relative error of at most 0.00002.
Values sent between devices are 32-bit elements; how exact they have to be, the bound alone decides.
No kernel may reach another device: no remote copies, remote signals or barrier semaphores. Data moves between devices by JAX's collectives and lax.ppermute only.
A program may use at most 64 MiB of HBM per device.

v0:
```python
import math

import jax
import jax.numpy as jnp
from jax import lax
from jax.sharding import PartitionSpec as P

REACH = 2
SLOTS = 4


time_step = 0.25
soften = 0.02
split_scale = 0.25


def shifted(shard, axis, by):
    length = lax.axis_size(axis)
    return lax.ppermute(shard, axis, [(i, (i + by) % length) for i in range(length)])


def pair_accel(target, source, weight):
    delta = source[:, :, None, :] - target[:, None, :, None]
    square = delta[0] * delta[0] + delta[1] * delta[1] + delta[2] * delta[2] + soften * soften
    inverse = lax.rsqrt(square)
    scaled = square * inverse / (2.0 * split_scale)
    factor = jax.scipy.special.erfc(scaled) + 2.0 / math.sqrt(math.pi) * scaled * jnp.exp(
        -scaled * scaled
    )
    strength = weight[:, None, :] * factor * inverse * inverse * inverse
    return jnp.sum(strength[None] * delta, axis=(1, 3))


def per_device(
    positions,
    velocities,
    masses,
    active_leaves,
    active_count,
    partner_owner,
    partner_leaf,
    mig_leaf,
):
    leaves = positions.shape[1]
    act_slots = active_leaves.shape[0]
    domains = lax.axis_size("dom")
    myself = lax.axis_index("dom")
    offsets = [o for o in range(-REACH, REACH + 1) if o != 0]
    relative = jnp.mod(partner_owner - myself + REACH, domains) - REACH
    source = jnp.concatenate([positions, masses[None]], axis=0)
    pieces = [source]
    for offset in offsets:
        pieces.append(shifted(source, "dom", -offset))
    buffer = jnp.concatenate(pieces, axis=1)
    side = jnp.where(relative < 0, relative + REACH, relative + REACH - 1) + 1
    lookup = jnp.where(relative == 0, partner_leaf, side * leaves + partner_leaf)
    gathered = jnp.moveaxis(buffer[:, lookup, :], 1, 0)

    def one_slot(pair):
        target_id, block = pair
        return pair_accel(positions[:, target_id, :], block[:3], block[3])

    accel = lax.map(one_slot, (active_leaves, gathered))
    live = jnp.arange(act_slots, dtype=jnp.int32) < active_count[0]
    accel = jnp.where(live[:, None, None], accel, jnp.float32(0.0))
    new_velocities = velocities.at[:, active_leaves, :].add(jnp.moveaxis(time_step * accel, 1, 0))
    new_positions = positions + time_step * new_velocities
    state = jnp.concatenate([new_positions, new_velocities, masses[None]], axis=0)
    table = mig_leaf.reshape(2 * REACH, SLOTS)
    blocks = state[:, jnp.maximum(table, 0), :]
    blocks = blocks * jnp.where(table >= 0, 1.0, 0.0).astype(jnp.float32)[None, :, :, None]
    received = []
    for number, offset in enumerate(offsets):
        received.append(shifted(blocks[:, number], "dom", offset))
    arrived = jnp.stack(received, axis=1).reshape(7, 2 * REACH * SLOTS, blocks.shape[-1])
    return (new_positions, new_velocities, arrived)


def solution(mesh):
    return jax.shard_map(
        per_device,
        mesh=mesh,
        in_specs=(
            P(None, "dom", None),
            P(None, "dom", None),
            P("dom", None),
            P("dom"),
            P("dom"),
            P("dom", None),
            P("dom", None),
            P("dom"),
        ),
        out_specs=(P(None, "dom", None), P(None, "dom", None), P(None, "dom", None)),
        check_vma=False,
    )
```

profile of v0, /device:TPU:1, one launch (start us, length us, event | category | flops | bytes accessed | tf_op | source)
XLA Modules:
  0.0 180.6 jit_solution(17688731359224586298)
XLA Ops:
  0.7 1.7 copy.31
  2.4 1.9 %constant_dynamic-update-slice_fusion.4 = (f32[4,2560,128]{2,0,1:T(4,128)}, f32[4,512,128]{2,0,1:T(4,128)}) fusion(f32[1,512,128]{2,0,1:T(1,128)S(1)} %bitcast.57, f32[3,512,128]{2,0,1:T(4,128)S(1)} %copy.31), kind=kLoop, calls=%fused_computation.54 | loop fusion | flops 262143 | bytes 3145728
  4.4 2.0 %collective-permute-start = (f32[4,512,128]{2,0,1:T(4,128)}, f32[4,512,128]{2,0,1:T(4,128)}, u32[]{:S(2)}, u32[]{:S(2)}) collective-permute-start(f32[4,512,128]{2,0,1:T(4,128)} %get-tuple-element.95), channel_id=1, source_target_pairs={{0,2},{1,3},{2,4},{3,5},{4,6},{5,7},{6,8},{7,9},{8,10},{9,11},{10,... | collective-permute-start | bytes 3145736 | tf_op jit(solution)/shard_map/ppermute | solution.py:19
  6.4 2.1 %collective-permute-start.1 = (f32[4,512,128]{2,0,1:T(4,128)}, f32[4,512,128]{2,0,1:T(4,128)}, u32[]{:S(2)}, u32[]{:S(2)}) collective-permute-start(f32[4,512,128]{2,0,1:T(4,128)} %get-tuple-element.95), channel_id=1, source_target_pairs={{0,1},{1,2},{2,3},{3,4},{4,5},{5,6},{6,7},{7,8},{8,9},{9,10},{10,1... | collective-permute-start | bytes 3145736 | tf_op jit(solution)/shard_map/ppermute | solution.py:19
  8.5 5.8 %collective-permute-start.3 = (f32[4,512,128]{2,0,1:T(4,128)}, f32[4,512,128]{2,0,1:T(4,128)}, u32[]{:S(2)}, u32[]{:S(2)}) collective-permute-start(f32[4,512,128]{2,0,1:T(4,128)} %get-tuple-element.95), channel_id=1, source_target_pairs={{0,126},{1,127},{2,0},{3,1},{4,2},{5,3},{6,4},{7,5},{8,6},{9,7},{1... | collective-permute-start | bytes 3145736 | tf_op jit(solution)/shard_map/ppermute | solution.py:19
  15.2 21.6 %collective-permute-done = f32[4,512,128]{2,0,1:T(4,128)} collective-permute-done((f32[4,512,128]{2,0,1:T(4,128)}, f32[4,512,128]{2,0,1:T(4,128)}, u32[]{:S(2)}, u32[]{:S(2)}) %collective-permute-start) | collective-permute-done | bytes 1048608 | tf_op jit(solution)/shard_map/ppermute | solution.py:19
  36.8 2.3 %constant_dynamic-update-slice_fusion.3 = f32[4,2560,128]{2,0,1:T(4,128)} fusion(f32[4,2560,128]{2,0,1:T(4,128)} %get-tuple-element.94, f32[4,512,128]{2,0,1:T(4,128)} %collective-permute-done), kind=kLoop, calls=%fused_computation.53 | loop fusion | bytes 2097152
  39.1 1.9 %collective-permute-done.1 = f32[4,512,128]{2,0,1:T(4,128)} collective-permute-done((f32[4,512,128]{2,0,1:T(4,128)}, f32[4,512,128]{2,0,1:T(4,128)}, u32[]{:S(2)}, u32[]{:S(2)}) %collective-permute-start.1) | collective-permute-done | bytes 1048608 | tf_op jit(solution)/shard_map/ppermute | solution.py:19
  40.9 2.3 %constant_dynamic-update-slice_fusion.2 = f32[4,2560,128]{2,0,1:T(4,128)} fusion(f32[4,2560,128]{2,0,1:T(4,128)} %constant_dynamic-update-slice_fusion.3, f32[4,512,128]{2,0,1:T(4,128)} %collective-permute-done.1), kind=kLoop, calls=%fused_computation.52 | loop fusion | bytes 2097152
  43.2 2.3 %constant_dynamic-update-slice_fusion.1 = f32[4,2560,128]{2,0,1:T(4,128)} fusion(f32[4,2560,128]{2,0,1:T(4,128)} %constant_dynamic-update-slice_fusion.2, f32[4,512,128]{2,0,1:T(4,128)} %collective-permute-done.2), kind=kLoop, calls=%fused_computation.51 | loop fusion | bytes 2097152
  45.5 2.3 %constant_dynamic-update-slice_fusion = f32[4,2560,128]{2,0,1:T(4,128)} fusion(f32[4,2560,128]{2,0,1:T(4,128)} %constant_dynamic-update-slice_fusion.1, f32[4,512,128]{2,0,1:T(4,128)} %collective-permute-done.3), kind=kLoop, calls=%fused_computation.50 | loop fusion | bytes 2097152 | tf_op jit(solution)/shard_map/concatenate | solution.py:54
  47.7 3.5 %gather_fusion = f32[256,4,128]{2,1,0:T(4,128)S(1)} fusion(f32[4,2560,128]{2,0,1:T(4,128)} %constant_dynamic-update-slice_fusion, s32[1024]{0:T(1024)S(1)} %pad_clamp_fusion.1), kind=kCustom, calls=%fused_computation | custom fusion | bytes 1049600 | tf_op jit(solution)/shard_map/gather | solution.py:57
  51.3 102.2 %while.13 = (s32[]{:T(128)}, f32[16,3,128]{2,0,1:T(8,128)S(1)}, f32[16,4,16,128]{3,2,0,1:T(8,128)S(1)}, s32[16]{0:T(128)S(1)}, f32[3,512,128]{2,0,1:T(4,128)S(1)}) while((s32[]{:T(128)}, f32[16,3,128]{2,0,1:T(8,128)S(1)}, f32[16,4,16,128]{3,2,0,1:T(8,128)S(1)}, s32[16]{0:T(128)S(1)}, f32[3,512,128]{2,0,1:T(4,128)S(1)}) %tuple.44), condition=%wide.region_2.3_spmd.clone, body=%wide.region_0.2_spmd.sunk.clone | while | flops 23330436 | bytes 8590967 | solution.py:63
  51.3 0.6 dynamic_slice.30
  54.3 2.8 %fusion.20 = f32[16,128,128]{2,1,0:T(8,128)S(1)} fusion(f32[3,16,128,128]{3,2,1,0:T(8,128)S(1)} %broadcast_subtract_fusion.3, f32[16,128]{1,0:T(8,128)S(1)} %slice_bitcast_fusion.11), kind=kLoop, calls=%fused_computation.14.clone.1.clone | loop fusion | flops 20185088 | bytes 4202496 | tf_op jit(solution)/shard_map/while/body/eval_jaxpr/mul | solution.py:31
  57.7 0.6 dynamic_slice.30
  60.7 2.8 %fusion.20 = f32[16,128,128]{2,1,0:T(8,128)S(1)} fusion(f32[3,16,128,128]{3,2,1,0:T(8,128)S(1)} %broadcast_subtract_fusion.3, f32[16,128]{1,0:T(8,128)S(1)} %slice_bitcast_fusion.11), kind=kLoop, calls=%fused_computation.14.clone.1.clone | loop fusion | flops 20185088 | bytes 4202496 | tf_op jit(solution)/shard_map/while/body/eval_jaxpr/mul | solution.py:31
  67.1 2.8 %fusion.20 = f32[16,128,128]{2,1,0:T(8,128)S(1)} fusion(f32[3,16,128,128]{3,2,1,0:T(8,128)S(1)} %broadcast_subtract_fusion.3, f32[16,128]{1,0:T(8,128)S(1)} %slice_bitcast_fusion.11), kind=kLoop, calls=%fused_computation.14.clone.1.clone | loop fusion | flops 20185088 | bytes 4202496 | tf_op jit(solution)/shard_map/while/body/eval_jaxpr/mul | solution.py:31
  70.5 0.6 dynamic_slice.30
  73.5 2.8 %fusion.20 = f32[16,128,128]{2,1,0:T(8,128)S(1)} fusion(f32[3,16,128,128]{3,2,1,0:T(8,128)S(1)} %broadcast_subtract_fusion.3, f32[16,128]{1,0:T(8,128)S(1)} %slice_bitcast_fusion.11), kind=kLoop, calls=%fused_computation.14.clone.1.clone | loop fusion | flops 20185088 | bytes 4202496 | tf_op jit(solution)/shard_map/while/body/eval_jaxpr/mul | solution.py:31
  76.9 0.6 dynamic_slice.30
  79.9 2.8 %fusion.20 = f32[16,128,128]{2,1,0:T(8,128)S(1)} fusion(f32[3,16,128,128]{3,2,1,0:T(8,128)S(1)} %broadcast_subtract_fusion.3, f32[16,128]{1,0:T(8,128)S(1)} %slice_bitcast_fusion.11), kind=kLoop, calls=%fused_computation.14.clone.1.clone | loop fusion | flops 20185088 | bytes 4202496 | tf_op jit(solution)/shard_map/while/body/eval_jaxpr/mul | solution.py:31
  86.3 2.8 %fusion.20 = f32[16,128,128]{2,1,0:T(8,128)S(1)} fusion(f32[3,16,128,128]{3,2,1,0:T(8,128)S(1)} %broadcast_subtract_fusion.3, f32[16,128]{1,0:T(8,128)S(1)} %slice_bitcast_fusion.11), kind=kLoop, calls=%fused_computation.14.clone.1.clone | loop fusion | flops 20185088 | bytes 4202496 | tf_op jit(solution)/shard_map/while/body/eval_jaxpr/mul | solution.py:31
  89.7 0.6 dynamic_slice.30
  92.7 2.8 %fusion.20 = f32[16,128,128]{2,1,0:T(8,128)S(1)} fusion(f32[3,16,128,128]{3,2,1,0:T(8,128)S(1)} %broadcast_subtract_fusion.3, f32[16,128]{1,0:T(8,128)S(1)} %slice_bitcast_fusion.11), kind=kLoop, calls=%fused_computation.14.clone.1.clone | loop fusion | flops 20185088 | bytes 4202496 | tf_op jit(solution)/shard_map/while/body/eval_jaxpr/mul | solution.py:31
  96.0 0.6 dynamic_slice.30
  99.1 2.8 %fusion.20 = f32[16,128,128]{2,1,0:T(8,128)S(1)} fusion(f32[3,16,128,128]{3,2,1,0:T(8,128)S(1)} %broadcast_subtract_fusion.3, f32[16,128]{1,0:T(8,128)S(1)} %slice_bitcast_fusion.11), kind=kLoop, calls=%fused_computation.14.clone.1.clone | loop fusion | flops 20185088 | bytes 4202496 | tf_op jit(solution)/shard_map/while/body/eval_jaxpr/mul | solution.py:31
  102.4 0.6 dynamic_slice.30
  105.4 2.8 %fusion.20 = f32[16,128,128]{2,1,0:T(8,128)S(1)} fusion(f32[3,16,128,128]{3,2,1,0:T(8,128)S(1)} %broadcast_subtract_fusion.3, f32[16,128]{1,0:T(8,128)S(1)} %slice_bitcast_fusion.11), kind=kLoop, calls=%fused_computation.14.clone.1.clone | loop fusion | flops 20185088 | bytes 4202496 | tf_op jit(solution)/shard_map/while/body/eval_jaxpr/mul | solution.py:31
  108.8 0.6 dynamic_slice.30
  111.8 2.8 %fusion.20 = f32[16,128,128]{2,1,0:T(8,128)S(1)} fusion(f32[3,16,128,128]{3,2,1,0:T(8,128)S(1)} %broadcast_subtract_fusion.3, f32[16,128]{1,0:T(8,128)S(1)} %slice_bitcast_fusion.11), kind=kLoop, calls=%fused_computation.14.clone.1.clone | loop fusion | flops 20185088 | bytes 4202496 | tf_op jit(solution)/shard_map/while/body/eval_jaxpr/mul | solution.py:31
  118.2 2.8 %fusion.20 = f32[16,128,128]{2,1,0:T(8,128)S(1)} fusion(f32[3,16,128,128]{3,2,1,0:T(8,128)S(1)} %broadcast_subtract_fusion.3, f32[16,128]{1,0:T(8,128)S(1)} %slice_bitcast_fusion.11), kind=kLoop, calls=%fused_computation.14.clone.1.clone | loop fusion | flops 20185088 | bytes 4202496 | tf_op jit(solution)/shard_map/while/body/eval_jaxpr/mul | solution.py:31
  121.6 0.6 dynamic_slice.30
  124.6 2.8 %fusion.20 = f32[16,128,128]{2,1,0:T(8,128)S(1)} fusion(f32[3,16,128,128]{3,2,1,0:T(8,128)S(1)} %broadcast_subtract_fusion.3, f32[16,128]{1,0:T(8,128)S(1)} %slice_bitcast_fusion.11), kind=kLoop, calls=%fused_computation.14.clone.1.clone | loop fusion | flops 20185088 | bytes 4202496 | tf_op jit(solution)/shard_map/while/body/eval_jaxpr/mul | solution.py:31
  128.0 0.6 dynamic_slice.30
  131.0 2.8 %fusion.20 = f32[16,128,128]{2,1,0:T(8,128)S(1)} fusion(f32[3,16,128,128]{3,2,1,0:T(8,128)S(1)} %broadcast_subtract_fusion.3, f32[16,128]{1,0:T(8,128)S(1)} %slice_bitcast_fusion.11), kind=kLoop, calls=%fused_computation.14.clone.1.clone | loop fusion | flops 20185088 | bytes 4202496 | tf_op jit(solution)/shard_map/while/body/eval_jaxpr/mul | solution.py:31
  137.4 2.8 %fusion.20 = f32[16,128,128]{2,1,0:T(8,128)S(1)} fusion(f32[3,16,128,128]{3,2,1,0:T(8,128)S(1)} %broadcast_subtract_fusion.3, f32[16,128]{1,0:T(8,128)S(1)} %slice_bitcast_fusion.11), kind=kLoop, calls=%fused_computation.14.clone.1.clone | loop fusion | flops 20185088 | bytes 4202496 | tf_op jit(solution)/shard_map/while/body/eval_jaxpr/mul | solution.py:31
  140.8 0.6 dynamic_slice.30
  143.8 2.8 %fusion.20 = f32[16,128,128]{2,1,0:T(8,128)S(1)} fusion(f32[3,16,128,128]{3,2,1,0:T(8,128)S(1)} %broadcast_subtract_fusion.3, f32[16,128]{1,0:T(8,128)S(1)} %slice_bitcast_fusion.11), kind=kLoop, calls=%fused_computation.14.clone.1.clone | loop fusion | flops 20185088 | bytes 4202496 | tf_op jit(solution)/shard_map/while/body/eval_jaxpr/mul | solution.py:31
  150.2 2.8 %fusion.20 = f32[16,128,128]{2,1,0:T(8,128)S(1)} fusion(f32[3,16,128,128]{3,2,1,0:T(8,128)S(1)} %broadcast_subtract_fusion.3, f32[16,128]{1,0:T(8,128)S(1)} %slice_bitcast_fusion.11), kind=kLoop, calls=%fused_computation.14.clone.1.clone | loop fusion | flops 20185088 | bytes 4202496 | tf_op jit(solution)/shard_map/while/body/eval_jaxpr/mul | solution.py:31
  153.6 1.5 scatter_fusion
  155.3 2.4 %copy.38 = f32[7,512,128]{2,0,1:T(8,128)} copy(f32[7,512,128]{2,1,0:T(8,128)S(1)} %pad_maximum_fusion) | data formatting | bytes 3670016 | tf_op jit(solution)/shard_map/concatenate | solution.py:68
  157.8 2.1 %gather_fusion.1 = f32[16,7,128]{2,1,0:T(8,128)S(1)} fusion(f32[7,512,128]{2,0,1:T(8,128)} %copy.38, s32[1024]{0:T(1024)S(1)} %pad_clamp_fusion), kind=kCustom, calls=%fused_computation.1 | custom fusion | bytes 114752 | tf_op jit(solution)/shard_map/gather | solution.py:70
  160.0 7.3 %collective-permute-start.4 = (f32[7,4,128]{2,0,1:T(8,128)S(1)}, f32[7,4,128]{2,0,1:T(8,128)S(1)}, u32[]{:S(2)}, u32[]{:S(2)}) collective-permute-start(f32[7,4,128]{2,0,1:T(8,128)S(1)} %get-tuple-element.96), channel_id=1, source_target_pairs={{0,126},{1,127},{2,0},{3,1},{4,2},{5,3},{6,4},{7,5},{8,6},{9,7},{1... | collective-permute-start | bytes 43016 | tf_op jit(solution)/shard_map/ppermute | solution.py:19
  167.3 4.4 %collective-permute-start.5 = (f32[7,4,128]{2,0,1:T(8,128)S(1)}, f32[7,4,128]{2,0,1:T(8,128)S(1)}, u32[]{:S(2)}, u32[]{:S(2)}) collective-permute-start(f32[7,4,128]{2,0,1:T(8,128)S(1)} %get-tuple-element.99), channel_id=1, source_target_pairs={{0,127},{1,0},{2,1},{3,2},{4,3},{5,4},{6,5},{7,6},{8,7},{9,8},{10,... | collective-permute-start | bytes 43016 | tf_op jit(solution)/shard_map/ppermute | solution.py:19
  171.7 0.8 collective-permute-done.5
  172.9 7.0 %collective-permute-done.7 = f32[7,4,128]{2,0,1:T(8,128)S(1)} collective-permute-done((f32[7,4,128]{2,0,1:T(8,128)S(1)}, f32[7,4,128]{2,0,1:T(8,128)S(1)}, u32[]{:S(2)}, u32[]{:S(2)}) %collective-permute-start.7) | collective-permute-done | bytes 14368 | tf_op jit(solution)/shard_map/ppermute | solution.py:19
  179.9 0.6 copy.39
  (175 shorter events, 19.1 us)
Async XLA Ops:
  0.6 1.8 copy-start.4
  0.6 14.6 %copy-start.8 = (s32[16]{0:T(128)S(1)}, s32[16]{0:T(128)}, u32[]{:S(2)}) copy-start(s32[16]{0:T(128)} %param.13) | copy-start | bytes 196
  0.7 13.6 %copy-start.6 = (s32[16,16]{1,0:T(8,128)S(1)}, s32[16,16]{1,0:T(8,128)}, u32[]{:S(2)}) copy-start(s32[16,16]{1,0:T(8,128)} %param.15) | copy-start | bytes 3076
  0.7 13.6 %copy-start.5 = (s32[16,16]{1,0:T(8,128)S(1)}, s32[16,16]{1,0:T(8,128)}, u32[]{:S(2)}) copy-start(s32[16,16]{1,0:T(8,128)} %param.16) | copy-start | bytes 3076
  0.7 14.4 %copy-start.7 = (s32[16]{0:T(128)S(1)}, s32[16]{0:T(128)}, u32[]{:S(2)}) copy-start(s32[16]{0:T(128)} %param.17) | copy-start | bytes 196
  4.4 32.4 %collective-permute-start = (f32[4,512,128]{2,0,1:T(4,128)}, f32[4,512,128]{2,0,1:T(4,128)}, u32[]{:S(2)}, u32[]{:S(2)}) collective-permute-start(f32[4,512,128]{2,0,1:T(4,128)} %get-tuple-element.95), channel_id=1, source_target_pairs={{0,2},{1,3},{2,4},{3,5},{4,6},{5,7},{6,8},{7,9},{8,10},{9,11},{10,... | collective-permute-start | bytes 3145736 | tf_op jit(solution)/shard_map/ppermute | solution.py:19
  6.4 34.5 %collective-permute-start.1 = (f32[4,512,128]{2,0,1:T(4,128)}, f32[4,512,128]{2,0,1:T(4,128)}, u32[]{:S(2)}, u32[]{:S(2)}) collective-permute-start(f32[4,512,128]{2,0,1:T(4,128)} %get-tuple-element.95), channel_id=1, source_target_pairs={{0,1},{1,2},{2,3},{3,4},{4,5},{5,6},{6,7},{7,8},{8,9},{9,10},{10,1... | collective-permute-start | bytes 3145736 | tf_op jit(solution)/shard_map/ppermute | solution.py:19
  8.5 34.7 %collective-permute-start.2 = (f32[4,512,128]{2,0,1:T(4,128)}, f32[4,512,128]{2,0,1:T(4,128)}, u32[]{:S(2)}, u32[]{:S(2)}) collective-permute-start(f32[4,512,128]{2,0,1:T(4,128)} %get-tuple-element.95), channel_id=1, source_target_pairs={{0,127},{1,0},{2,1},{3,2},{4,3},{5,4},{6,5},{7,6},{8,7},{9,8},{10,... | collective-permute-start | bytes 3145736 | tf_op jit(solution)/shard_map/ppermute | solution.py:19
  8.5 37.0 %collective-permute-start.3 = (f32[4,512,128]{2,0,1:T(4,128)}, f32[4,512,128]{2,0,1:T(4,128)}, u32[]{:S(2)}, u32[]{:S(2)}) collective-permute-start(f32[4,512,128]{2,0,1:T(4,128)} %get-tuple-element.95), channel_id=1, source_target_pairs={{0,126},{1,127},{2,0},{3,1},{4,2},{5,3},{6,4},{7,5},{8,6},{9,7},{1... | collective-permute-start | bytes 3145736 | tf_op jit(solution)/shard_map/ppermute | solution.py:19
  51.3 102.3 %copy-start.1 = (f32[3,512,128]{2,1,0:T(8,128)S(1)}, f32[3,512,128]{2,1,0:T(8,128)}, u32[]{:S(2)}) copy-start(f32[3,512,128]{2,1,0:T(8,128)} %param.11) | copy-start | bytes 2359300
  51.3 103.8 %copy-start.2 = (f32[3,512,128]{2,1,0:T(8,128)S(1)}, f32[3,512,128]{2,1,0:T(8,128)}, u32[]{:S(2)}) copy-start(f32[3,512,128]{2,1,0:T(8,128)} %param.10) | copy-start | bytes 2359300
  155.1 2.7 %copy-start = (f32[3,512,128]{2,1,0:T(8,128)}, f32[3,512,128]{2,1,0:T(8,128)S(1)}, u32[]{:S(2)}) copy-start(f32[3,512,128]{2,1,0:T(8,128)S(1)} %scatter_fusion) | copy-start | bytes 2359300
  155.2 2.6 %copy-start.3 = (f32[3,512,128]{2,1,0:T(8,128)}, f32[3,512,128]{2,1,0:T(8,128)S(1)}, u32[]{:S(2)}) copy-start(f32[3,512,128]{2,1,0:T(8,128)S(1)} %multiply_add_fusion) | copy-start | bytes 2359300
  160.0 11.7 %collective-permute-start.4 = (f32[7,4,128]{2,0,1:T(8,128)S(1)}, f32[7,4,128]{2,0,1:T(8,128)S(1)}, u32[]{:S(2)}, u32[]{:S(2)}) collective-permute-start(f32[7,4,128]{2,0,1:T(8,128)S(1)} %get-tuple-element.96), channel_id=1, source_target_pairs={{0,126},{1,127},{2,0},{3,1},{4,2},{5,3},{6,4},{7,5},{8,6},{9,7},{1... | collective-permute-start | bytes 43016 | tf_op jit(solution)/shard_map/ppermute | solution.py:19
  167.3 5.2 %collective-permute-start.5 = (f32[7,4,128]{2,0,1:T(8,128)S(1)}, f32[7,4,128]{2,0,1:T(8,128)S(1)}, u32[]{:S(2)}, u32[]{:S(2)}) collective-permute-start(f32[7,4,128]{2,0,1:T(8,128)S(1)} %get-tuple-element.99), channel_id=1, source_target_pairs={{0,127},{1,0},{2,1},{3,2},{4,3},{5,4},{6,5},{7,6},{8,7},{9,8},{10,... | collective-permute-start | bytes 43016 | tf_op jit(solution)/shard_map/ppermute | solution.py:19
  171.7 1.2 collective-permute-start.6
  171.7 8.2 %collective-permute-start.7 = (f32[7,4,128]{2,0,1:T(8,128)S(1)}, f32[7,4,128]{2,0,1:T(8,128)S(1)}, u32[]{:S(2)}, u32[]{:S(2)}) collective-permute-start(f32[7,4,128]{2,0,1:T(8,128)S(1)} %get-tuple-element.97), channel_id=1, source_target_pairs={{0,2},{1,3},{2,4},{3,5},{4,6},{5,7},{6,8},{7,9},{8,10},{9,11},{10,... | collective-permute-start | bytes 43016 | tf_op jit(solution)/shard_map/ppermute | solution.py:19
where the time goes:
time: 182 us; the launch traced here: 181 us
  other arithmetic  63.1 us (35%)
  loops' own time  32.3 us (18%)
  waiting for transfers between devices  31.6 us (17%)
  local copies, waits for them, and re-layouts  30.4 us (17%)
  starting transfers between devices  21.6 us (12%)
    mul x16, other arithmetic, pair_accel(): return jnp.sum(strength[None] * delta, axis=(1, 3))  45.5 us
    another operation x1, loops' own time, per_device(): accel = lax.map(one_slot, (active_leaves, gathered))  32.3 us
    ppermute x8, waiting for transfers between devices, shifted(): lax.ppermute(shard, axis, [(i, (i + by) % length) for i in range(length)])  31.6 us
    ppermute x8, starting transfers between devices, shifted(): lax.ppermute(shard, axis, [(i, (i + by) % length) for i in range(length)])  21.6 us
    dynamic_slice x32, local copies, waits for them, and re-layouts, per_device(): accel = lax.map(one_slot, (active_leaves, gathered))  9.57 us
    unnamed x22, local copies, waits for them, and re-layouts  8.62 us
    reduce_sum x16, other arithmetic, pair_accel(): return jnp.sum(strength[None] * delta, axis=(1, 3))  7.35 us
    sub x16, other arithmetic, pair_accel(): delta = source[:, :, None, :] - target[:, None, :, None]  6.53 us
  transfers between devices with their start and end apart: 8, of which 5 were waited for; matrix products, arithmetic and copies ran while one was open for 4% of the time, Pallas kernels for 0%

commit v1 on v0

v1 whole, which is shorter than its diff:
```python
import functools
import math

import jax
import jax.numpy as jnp
from jax import lax
from jax.experimental import pallas as pl
from jax.experimental.pallas import tpu as pltpu
from jax.sharding import PartitionSpec as P

REACH = 2
SLOTS = 4
IMPORT = 8
ACT = 16
PARTNERS = 16
LANES = 128
SIDES = 2 * REACH
IMPORTS = SIDES * IMPORT
BIG = 1 << 20
OFFSETS = [o for o in range(-REACH, REACH + 1) if o != 0]

soften = 0.02
EPS = 4.0 * soften * soften
NEG_LOG2E = -math.log2(math.e)
TWO_OVER_ROOT_PI = 2.0 / math.sqrt(math.pi)

REMOTE, LOCAL, N_REMOTE, N_LOCAL, ORDER, COUNTS, FROM = 0, 256, 512, 528, 544, 560, 576
PLAN = 592

VMEM = pl.BlockSpec(memory_space=pltpu.VMEM)
SMEM = pl.BlockSpec(memory_space=pltpu.SMEM)
F32, I32 = jnp.float32, jnp.int32


def params(mib):
    return pltpu.CompilerParams(vmem_limit_bytes=mib << 20)


def shifted(shard, by):
    length = lax.axis_size("dom")
    return lax.ppermute(shard, "dom", [(i, (i + by) % length) for i in range(length)])


def request_kernel(domains, me_ref, owner_ref, leaf_ref, *outs):
    requests, map_ref, mult_ref = outs[:SIDES], outs[SIDES], outs[SIDES + 1]
    leaf = leaf_ref[...]
    relative = owner_ref[...] - me_ref[0] + REACH
    relative = jnp.where(relative < 0, relative + domains, relative)
    relative = jnp.where(relative >= domains, relative - domains, relative)
    lane = lax.broadcasted_iota(I32, (1, LANES), 1)
    place = IMPORTS + leaf
    for side, offset in enumerate(OFFSETS):
        mine = relative == offset + REACH
        key = jnp.where(mine, leaf, BIG)
        rank = jnp.zeros_like(leaf)
        row = jnp.zeros((1, LANES), I32)
        for k in range(IMPORT):
            least = jnp.min(jnp.min(key, axis=0, keepdims=True), axis=1, keepdims=True)
            row = jnp.where(lane == k, jnp.broadcast_to(least, row.shape), row)
            here = key == least
            rank = jnp.where(here, k, rank)
            key = jnp.where(here, BIG, key)
        requests[side][...] = jnp.minimum(row, 511)
        place = jnp.where(mine, side * IMPORT + rank, place)
    map_ref[...] = place
    column = lax.broadcasted_iota(I32, place.shape, 1)
    times = jnp.zeros_like(place)
    earlier = jnp.zeros_like(place)
    for k in range(PARTNERS):
        same = (place == place[:, k : k + 1]).astype(I32)
        times = times + same
        earlier = jnp.where(column > k, earlier + same, earlier)
    mult_ref[...] = jnp.where(earlier > 0, 0, times)


def plan_kernel(map_ref, mult_ref, active_ref, count_ref, mig_ref, plan_ref):
    live = count_ref[0]

    def one_slot(a, tally):
        first, last = tally

        def entry(k, sizes):
            n_remote, n_local = sizes
            place = map_ref[a, k]
            times = mult_ref[a, k]
            is_remote = place < IMPORTS
            word = place * 32 + times
            plan_ref[REMOTE + a * PARTNERS + n_remote] = word
            plan_ref[LOCAL + a * PARTNERS + n_local] = word - IMPORTS * 32
            counts = times > 0
            return (
                n_remote + jnp.where(counts & is_remote, 1, 0),
                n_local + jnp.where(counts & ~is_remote, 1, 0),
            )

        sizes = (jnp.int32(0), jnp.int32(0))
        for k in range(PARTNERS - 1):
            sizes = entry(k, sizes)
        k = PARTNERS - 1
        n_remote, n_local = sizes
        place, times = map_ref[a, k], mult_ref[a, k]
        remote_last = (times > 0) & (place < IMPORTS)
        local_last = (times > 0) & (place >= IMPORTS)

        @pl.when(remote_last)
        def _():
            plan_ref[REMOTE + a * PARTNERS + n_remote] = place * 32 + times

        @pl.when(local_last)
        def _():
            plan_ref[LOCAL + a * PARTNERS + n_local] = (place - IMPORTS) * 32 + times

        plan_ref[N_REMOTE + a] = n_remote + jnp.where(remote_last, 1, 0)
        plan_ref[N_LOCAL + a] = n_local + jnp.where(local_last, 1, 0)
        leaf = active_ref[a]
        leaves_home = jnp.int32(0)
        for n in range(SIDES * SLOTS):
            hit = mig_ref[n] == leaf
            leaves_home = leaves_home | jnp.where(hit, 1, 0)

            @pl.when(hit)
            def _():
                plan_ref[FROM + n] = a

        plan_ref[ORDER + jnp.where(leaves_home > 0, first, last)] = a
        return (first + leaves_home, last - (1 - leaves_home))

    for n in range(SIDES * SLOTS):
        plan_ref[FROM + n] = -1
    first, _ = lax.fori_loop(0, live, one_slot, (jnp.int32(0), live - 1))
    plan_ref[COUNTS] = first
    plan_ref[COUNTS + 1] = live


def reply_kernel(r0, r1, r2, r3, positions_ref, masses_ref, o0, o1, o2, o3):
    for request, out in ((r0, o0), (r1, o1), (r2, o2), (r3, o3)):
        for k in range(IMPORT):
            leaf = request[0, k]
            for c in range(3):
                out[4 * k + c : 4 * k + c + 1, :] = 2.0 * positions_ref[c, pl.ds(leaf, 1), :]
            out[4 * k + 3 : 4 * k + 4, :] = masses_ref[pl.ds(leaf, 1), :]


def set_targets(targets, positions_ref, leaf):
    for c in range(3):
        row = 2.0 * positions_ref[c, pl.ds(leaf, 1), :]
        targets[c] = jnp.transpose(jnp.broadcast_to(row, (LANES, LANES)))


def add_pairs(targets, total, sources):
    wide = [[jnp.broadcast_to(v, (8, LANES)) for v in source] for source in sources]
    for g in range(LANES // 8):
        rows = slice(8 * g, 8 * g + 8)
        tx, ty, tz = (targets[c, rows, :] for c in range(3))
        ax = ay = az = None
        for x, y, z, m, mc in wide:
            dx, dy, dz = x - tx, y - ty, z - tz
            square = dx * dx + dy * dy + (dz * dz + EPS)
            inverse = lax.rsqrt(square)
            gauss = mc * jnp.exp2(square * NEG_LOG2E)
            tail = (1.0 - lax.erf(square * inverse)) * (m * inverse)
            strength = (tail + gauss) * (inverse * inverse)
            px, py, pz = strength * dx, strength * dy, strength * dz
            ax, ay, az = (px, py, pz) if ax is None else (ax + px, ay + py, az + pz)
        total[0, rows, :] += ax
        total[1, rows, :] += ay
        total[2, rows, :] += az


def add_list(targets, total, plan_ref, base, n, row_of):
    def some(start, many):
        sources = []
        for q in range(many):
            word = plan_ref[base + start + q]
            x, y, z, m = row_of(lax.shift_right_logical(word, 5))
            m = m * (word & 31).astype(F32)
            sources.append((x, y, z, m, m * TWO_OVER_ROOT_PI))
        add_pairs(targets, total, sources)

    fours = lax.shift_right_logical(n, 2)

    @pl.loop(0, fours)
    def _(q):
        some(4 * q, 4)

    @pl.when((n & 2) > 0)
    def _():
        some(4 * fours, 2)

    @pl.when((n & 1) > 0)
    def _():
        some(n - 1, 1)


def lane_sums(total):
    ones = jnp.ones((8, LANES), F32)
    return [
        lax.dot_general(
            ones,
            total[c],
            (((1,), (1,)), ((), ())),
            precision=lax.Precision.HIGHEST,
            preferred_element_type=F32,
        )[0:1]
        for c in range(3)
    ]


def local_kernel(plan_ref, active_ref, positions_ref, masses_ref, _, kick_ref, targets, total):
    kick_ref[...] = jnp.zeros_like(kick_ref)

    def row_of(leaf):
        at = pl.ds(leaf, 1)
        return [2.0 * positions_ref[c, at, :] for c in range(3)] + [masses_ref[at, :]]

    @pl.loop(0, plan_ref[COUNTS + 1])
    def _(a):
        n = plan_ref[N_LOCAL + a]

        @pl.when(n > 0)
        def _():
            set_targets(targets, positions_ref, active_ref[a])
            total[...] = jnp.zeros_like(total)
            add_list(targets, total, plan_ref, LOCAL + a * PARTNERS, n, row_of)
            for c, row in enumerate(lane_sums(total)):
                kick_ref[a, c : c + 1, :] = row


def remote_slots(lo, hi, plan_ref, active_ref, positions_ref, imports, kick_ref, targets, total):
    def row_of(place):
        return [imports[pl.ds(4 * place + c, 1), :] for c in range(4)]

    @pl.loop(lo, hi)
    def _(q):
        a = plan_ref[ORDER + q]
        set_targets(targets, positions_ref, active_ref[a])
        total[...] = jnp.zeros_like(total)
        add_list(targets, total, plan_ref, REMOTE + a * PARTNERS, plan_ref[N_REMOTE + a], row_of)
        for c, row in enumerate(lane_sums(total)):
            kick_ref[a, c : c + 1, :] += row


def gather_imports(received, imports):
    for side, ref in enumerate(received):
        imports[side * 4 * IMPORT : (side + 1) * 4 * IMPORT, :] = ref[...]


def leaving_kernel(plan_ref, active_ref, mig_ref, positions_ref, velocities_ref, masses_ref, kick_in, r0, r1, r2, r3,
                   kick_ref, b0, b1, b2, b3, imports, targets, total):
    gather_imports((r0, r1, r2, r3), imports)
    kick_ref[...] = kick_in[...]
    remote_slots(0, plan_ref[COUNTS], plan_ref, active_ref, positions_ref, imports, kick_ref, targets, total)
    for side, block in enumerate((b0, b1, b2, b3)):
        for k in range(SLOTS):
            n = side * SLOTS + k
            leaf = mig_ref[n]
            at = pl.ds(jnp.maximum(leaf, 0), 1)
            held = jnp.full((1, LANES), jnp.where(leaf >= 0, 1, 0), I32) > 0
            a = plan_ref[FROM + n]
            kicked = jnp.full((1, LANES), jnp.where(a >= 0, 1, 0), I32) > 0
            for c in range(3):
                kick = jnp.where(kicked, kick_ref[jnp.maximum(a, 0), c : c + 1, :], 0.0)
                v = velocities_ref[c, at, :] + kick
                x = positions_ref[c, at, :] + 0.25 * v
                block[c, k : k + 1, :] = jnp.where(held, x, 0.0)
                block[3 + c, k : k + 1, :] = jnp.where(held, v, 0.0)
            block[6, k : k + 1, :] = jnp.where(held, masses_ref[at, :], 0.0)


def staying_kernel(plan_ref, active_ref, positions_ref, velocities_ref, kick_in, r0, r1, r2, r3,
                   new_positions, new_velocities, kick_ref, imports, targets, total):
    gather_imports((r0, r1, r2, r3), imports)
    kick_ref[...] = kick_in[...]
    new_velocities[...] = velocities_ref[...]
    new_positions[...] = positions_ref[...] + 0.25 * velocities_ref[...]
    live = plan_ref[COUNTS + 1]
    remote_slots(plan_ref[COUNTS], live, plan_ref, active_ref, positions_ref, imports, kick_ref, targets, total)

    @pl.loop(0, live)
    def _(a):
        at = pl.ds(active_ref[a], 1)
        for c in range(3):
            v = velocities_ref[c, at, :] + kick_ref[a, c : c + 1, :]
            new_velocities[c, at, :] = v
            new_positions[c, at, :] = positions_ref[c, at, :] + 0.25 * v


def shape(*dims, dtype=F32):
    return jax.ShapeDtypeStruct(dims, dtype)


def per_device(positions, velocities, masses, active_leaves, active_count, partner_owner, partner_leaf, mig_leaf):
    leaves = positions.shape[1]
    domains = lax.axis_size("dom")
    me = lax.axis_index("dom").astype(I32).reshape(1)
    *requests, place, times = pl.pallas_call(
        functools.partial(request_kernel, domains),
        out_shape=[shape(1, LANES, dtype=I32)] * SIDES + [shape(ACT, PARTNERS, dtype=I32)] * 2,
        in_specs=[SMEM, VMEM, VMEM],
        out_specs=[VMEM] * (SIDES + 2),
        compiler_params=params(4),
        name="requests",
    )(me, partner_owner, partner_leaf)
    asked = [shifted(r, o) for r, o in zip(requests, OFFSETS)]
    plan = pl.pallas_call(
        plan_kernel,
        out_shape=shape(PLAN, dtype=I32),
        in_specs=[SMEM] * 5,
        out_specs=SMEM,
        compiler_params=params(4),
        cost_estimate=pl.CostEstimate(flops=10_000_000, bytes_accessed=10_000, transcendentals=0),
        name="plan",
    )(place, times, active_leaves, active_count, mig_leaf)
    replies = pl.pallas_call(
        reply_kernel,
        out_shape=[shape(4 * IMPORT, LANES)] * SIDES,
        in_specs=[SMEM] * SIDES + [VMEM] * 2,
        out_specs=[VMEM] * SIDES,
        compiler_params=params(4),
        name="replies",
    )(*asked, positions, masses)
    received = [shifted(r, -o) for r, o in zip(replies, OFFSETS)]
    pair_scratch = [pltpu.VMEM((3, LANES, LANES), F32), pltpu.VMEM((3, LANES, LANES), F32)]
    kicks = pl.pallas_call(
        local_kernel,
        out_shape=shape(ACT, 8, LANES),
        in_specs=[SMEM, SMEM, VMEM, VMEM, pl.BlockSpec(memory_space=pl.ANY)],
        out_specs=VMEM,
        scratch_shapes=pair_scratch,
        compiler_params=params(8),
        cost_estimate=pl.CostEstimate(flops=10_000_000, bytes_accessed=10_000, transcendentals=0),
        name="local_pairs",
    )(plan, active_leaves, positions, masses, replies[0])
    imports = [pltpu.VMEM((4 * IMPORTS, LANES), F32)]
    kicks, *blocks = pl.pallas_call(
        leaving_kernel,
        out_shape=[shape(ACT, 8, LANES)] + [shape(7, SLOTS, LANES)] * SIDES,
        in_specs=[SMEM] * 3 + [VMEM] * (4 + SIDES),
        out_specs=[VMEM] * (1 + SIDES),
        scratch_shapes=imports + pair_scratch,
        compiler_params=params(8),
        name="leaving",
    )(plan, active_leaves, mig_leaf, positions, velocities, masses, kicks, *received)
    arrived = [shifted(b, o) for b, o in zip(blocks, OFFSETS)]
    new_positions, new_velocities = pl.pallas_call(
        staying_kernel,
        out_shape=[shape(3, leaves, LANES)] * 2,
        in_specs=[SMEM] * 2 + [VMEM] * (3 + SIDES),
        out_specs=[VMEM] * 2,
        scratch_shapes=[pltpu.VMEM((ACT, 8, LANES), F32)] + imports + pair_scratch,
        compiler_params=params(16),
        cost_estimate=pl.CostEstimate(flops=100_000_000, bytes_accessed=10_000, transcendentals=0),
        name="staying",
    )(plan, active_leaves, positions, velocities, kicks, *received)
    arrived = jnp.concatenate(arrived, axis=1)
    return new_positions, new_velocities, arrived


def solution(mesh):
    return jax.shard_map(
        per_device,
        mesh=mesh,
        in_specs=(
            P(None, "dom", None),
            P(None, "dom", None),
            P("dom", None),
            P("dom"),
            P("dom"),
            P("dom", None),
            P("dom", None),
            P("dom"),
        ),
        out_specs=(P(None, "dom", None), P(None, "dom", None), P(None, "dom", None)),
        check_vma=False,
    )
```

time: 182 us -> 62.4 us (0.34); the launches traced: 181 us -> 63 us
  other arithmetic: 63.1 us -> 0.64 us
  loops' own time: 32.3 us -> 0 us
  local copies, waits for them, and re-layouts: 30.4 us -> 3.49 us
  waiting for transfers between devices: 31.6 us -> 7.86 us
  Pallas kernels: 0 us -> 22.1 us
  starting transfers between devices: 21.6 us -> 27.5 us
    mul x18 -> x0, other arithmetic: 45.6 us -> none  [the longest x16 45.5 us: pair_accel(): return jnp.sum(strength[None] * delta, axis=(1, 3))]
    another operation x1 -> x0, loops' own time: 32.3 us -> none  [per_device(): accel = lax.map(one_slot, (active_leaves, gathered))]
    ppermute x8 -> x12, waiting for transfers between devices: 31.6 us -> 7.86 us  [shifted(): lax.ppermute(shard, 'dom', [(i, (i + by) % length) for i in range(length)])]
    pallas_call x0 -> x6, Pallas kernels: none -> 22.1 us  [the longest x1 11.1 us: per_device(): pl.pallas_call(staying_kernel, out_shape=[shape(3, leaves, LANES)] * 2, i...]
    dynamic_slice x32 -> x0, local copies, waits for them, and re-layouts: 9.57 us -> none  [per_device(): accel = lax.map(one_slot, (active_leaves, gathered))]
    reduce_sum x16 -> x0, other arithmetic: 7.35 us -> none  [pair_accel(): return jnp.sum(strength[None] * delta, axis=(1, 3))]
    sub x16 -> x0, other arithmetic: 6.53 us -> none  [pair_accel(): delta = source[:, :, None, :] - target[:, None, :, None]]
    ppermute x8 -> x12, starting transfers between devices: 21.6 us -> 27.5 us  [shifted(): lax.ppermute(shard, 'dom', [(i, (i + by) % length) for i in range(length)])]
  transfers between devices with their start and end apart: 8 -> 12, of which waited for: 5 -> 2; matrix products, arithmetic and copies ran while one was open for 4% -> 0% of each run, Pallas kernels for 0% -> 31%
where the time goes in v1:
time: 62.4 us; the launch traced here: 63 us
  starting transfers between devices  27.5 us (44%)
  Pallas kernels  22.1 us (35%)
  waiting for transfers between devices  7.86 us (13%)
  local copies, waits for them, and re-layouts  3.49 us (6%)
  between operations  1.43 us (2%)
  other arithmetic  0.64 us (1%)
    ppermute x12, starting transfers between devices, shifted(): lax.ppermute(shard, 'dom', [(i, (i + by) % length) for i in range(length)])  27.5 us
    pallas_call x1, Pallas kernels, per_device(): pl.pallas_call(staying_kernel, out_shape=[shape(3, leaves, LANES)] * 2, i...  11.1 us
    ppermute x12, waiting for transfers between devices, shifted(): lax.ppermute(shard, 'dom', [(i, (i + by) % length) for i in range(length)])  7.86 us
    pallas_call x1, Pallas kernels, per_device(): pl.pallas_call(local_kernel, out_shape=shape(ACT, 8, LANES), in_specs=[SM...  5.87 us
    unnamed x18, local copies, waits for them, and re-layouts  3.49 us
    pallas_call x1, Pallas kernels, per_device(): pl.pallas_call(plan_kernel, out_shape=shape(PLAN, dtype=I32), in_specs=[S...  2.36 us
    pallas_call x1, Pallas kernels, per_device(): pl.pallas_call(functools.partial(request_kernel, domains), out_shape=[sha...  1.48 us
  transfers between devices with their start and end apart: 12, of which 2 were waited for; matrix products, arithmetic and copies ran while one was open for 0% of the time, Pallas kernels for 31%

profile of v1, /device:TPU:1, one launch (start us, length us, event | category | flops | bytes accessed | tf_op | source)
XLA Modules:
  0.0 63.0 jit_solution(1898026986396219428)
XLA Ops:
  0.6 0.0 copy-start.5
  0.6 0.7 %copy-done.5 = s32[16,16]{1,0:T(8,128)S(1)} copy-done((s32[16,16]{1,0:T(8,128)S(1)}, s32[16,16]{1,0:T(8,128)}, u32[]{:S(2)}) %copy-start.5) | copy-done | bytes 1048
  1.3 0.0 copy-start.6
  1.3 0.7 %copy-done.6 = s32[16,16]{1,0:T(8,128)S(1)} copy-done((s32[16,16]{1,0:T(8,128)S(1)}, s32[16,16]{1,0:T(8,128)}, u32[]{:S(2)}) %copy-start.6) | copy-done | bytes 1048
  2.0 1.5 %requests.1 = (s32[1,128]{1,0:T(1,128)S(1)}, s32[1,128]{1,0:T(1,128)S(1)}, s32[1,128]{1,0:T(1,128)S(1)}, s32[1,128]{1,0:T(1,128)S(1)}, s32[16,16]{1,0:T(8,128)S(1)}, /*index=5*/s32[16,16]{1,0:T(8,128)S(1)}) custom-call(s32[1]{0:T(128)} %bitcast.me_ref, s32[16,16]{1,0:T(8,128)S(1)} %copy-done.5, s32[16,16]{1,0:T(8,128)S(1)} %copy-done.6), custom_call_target="tpu_custom_call" | custom-call | tf_op jit(solution)/shard_map/requests/pallas_call | solution.py:296
  3.5 9.3 %collective-permute-start = (s32[1,128]{1,0:T(1,128)S(1)}, s32[1,128]{1,0:T(1,128)S(1)}, u32[]{:S(2)}, u32[]{:S(2)}) collective-permute-start(s32[1,128]{1,0:T(1,128)S(1)} %get-tuple-element.22), channel_id=1, source_target_pairs={{0,126},{1,127},{2,0},{3,1},{4,2},{5,3},{6,4},{7,5},{8,6},{9,7},{1... | collective-permute-start | bytes 1544 | tf_op jit(solution)/shard_map/ppermute | solution.py:41
  12.8 1.0 %collective-permute-start.1 = (s32[1,128]{1,0:T(1,128)S(1)}, s32[1,128]{1,0:T(1,128)S(1)}, u32[]{:S(2)}, u32[]{:S(2)}) collective-permute-start(s32[1,128]{1,0:T(1,128)S(1)} %get-tuple-element.23), channel_id=1, source_target_pairs={{0,127},{1,0},{2,1},{3,2},{4,3},{5,4},{6,5},{7,6},{8,7},{9,8},{10,... | collective-permute-start | bytes 1544 | tf_op jit(solution)/shard_map/ppermute | solution.py:41
  13.8 0.8 %collective-permute-start.2 = (s32[1,128]{1,0:T(1,128)S(1)}, s32[1,128]{1,0:T(1,128)S(1)}, u32[]{:S(2)}, u32[]{:S(2)}) collective-permute-start(s32[1,128]{1,0:T(1,128)S(1)} %get-tuple-element.24), channel_id=1, source_target_pairs={{0,1},{1,2},{2,3},{3,4},{4,5},{5,6},{6,7},{7,8},{8,9},{9,10},{10,1... | collective-permute-start | bytes 1544 | tf_op jit(solution)/shard_map/ppermute | solution.py:41
  14.6 0.0 collective-permute-start.3
  14.6 0.0 collective-permute-done.r0
  14.6 1.2 %collective-permute-done.1.r1 = s32[1,128]{1,0:T(1,128)S(1)} collective-permute-done((s32[1,128]{1,0:T(1,128)S(1)}, s32[1,128]{1,0:T(1,128)S(1)}, u32[]{:S(2)}, u32[]{:S(2)}) %collective-permute-start.1) | collective-permute-done | bytes 544 | tf_op jit(solution)/shard_map/ppermute | solution.py:41
  15.8 0.0 collective-permute-done.2.r2
  15.8 6.6 %collective-permute-done.3.r3 = s32[1,128]{1,0:T(1,128)S(1)} collective-permute-done((s32[1,128]{1,0:T(1,128)S(1)}, s32[1,128]{1,0:T(1,128)S(1)}, u32[]{:S(2)}, u32[]{:S(2)}) %collective-permute-start.3) | collective-permute-done | bytes 544 | tf_op jit(solution)/shard_map/ppermute | solution.py:41
  22.4 0.0 copy-start
  22.4 1.1 %copy-done = f32[3,512,128]{2,1,0:T(8,128)S(1)} copy-done((f32[3,512,128]{2,1,0:T(8,128)S(1)}, f32[3,512,128]{2,1,0:T(8,128)}, u32[]{:S(2)}) %copy-start) | copy-done | bytes 786456
  23.5 0.0 copy-start.3
  23.5 0.9 %copy-done.3 = f32[512,128]{1,0:T(8,128)S(1)} copy-done((f32[512,128]{1,0:T(8,128)S(1)}, f32[512,128]{1,0:T(8,128)}, u32[]{:S(2)}) %copy-start.3) | copy-done | bytes 262168
  24.5 0.0 copy-start.7
  24.5 0.0 copy-start.8
  24.5 0.0 copy-start.1
  24.5 0.6 %replies.1 = (f32[32,128]{1,0:T(8,128)S(1)}, f32[32,128]{1,0:T(8,128)S(1)}, f32[32,128]{1,0:T(8,128)S(1)}, f32[32,128]{1,0:T(8,128)S(1)}) custom-call(s32[1,128]{1,0:T(1,128)S(1)} %collective-permute-done.r0, s32[1,128]{1,0:T(1,128)S(1)} %collective-permute-done.1.r1, s32[1,128]{1,0:T(1,128)S(1)} %collective-permute-done.2.r2, ...), custom_call_target="tpu_custom_call" | custom-call | tf_op jit(solution)/shard_map/replies/pallas_call | solution.py:314
  25.1 0.0 copy-start.2
  25.1 0.1 collective-permute-start.5
  25.2 1.0 %collective-permute-start.6 = (f32[32,128]{1,0:T(8,128)S(1)}, f32[32,128]{1,0:T(8,128)S(1)}, u32[]{:S(2)}, u32[]{:S(2)}) collective-permute-start(f32[32,128]{1,0:T(8,128)S(1)} %get-tuple-element.28), channel_id=1, source_target_pairs={{0,127},{1,0},{2,1},{3,2},{4,3},{5,4},{6,5},{7,6},{8,7},{9,8},{10,... | collective-permute-start | bytes 49160 | tf_op jit(solution)/shard_map/ppermute | solution.py:41
  26.2 6.7 %collective-permute-start.7 = (f32[32,128]{1,0:T(8,128)S(1)}, f32[32,128]{1,0:T(8,128)S(1)}, u32[]{:S(2)}, u32[]{:S(2)}) collective-permute-start(f32[32,128]{1,0:T(8,128)S(1)} %get-tuple-element.29), channel_id=1, source_target_pairs={{0,126},{1,127},{2,0},{3,1},{4,2},{5,3},{6,4},{7,5},{8,6},{9,7},{1... | collective-permute-start | bytes 49160 | tf_op jit(solution)/shard_map/ppermute | solution.py:41
  32.9 0.0 collective-permute-start.4
  33.6 0.0 copy-done.7
  33.6 0.0 copy-done.8
  33.6 2.4 %plan.1.plan_ref = s32[592]{0:T(1024)S(1)} custom-call(s32[16,16]{1,0:T(8,128)S(1)} %get-tuple-element.20.map_ref, s32[16,16]{1,0:T(8,128)S(1)} %get-tuple-element.21.mult_ref, s32[16]{0:T(128)S(1)} %copy-done.7, s32[1]{0:T(128)S(6)} %copy.11.count_ref, s32[16]{0:T(128)S(1)} %copy-done.8), custom_call_target="tpu_custom_call" | custom-call | flops 10000000 | bytes 10000 | tf_op jit(solution)/shard_map/plan/pallas_call | solution.py:305
  36.0 0.0 copy-done.1
  36.0 0.0 copy-done.4
  36.0 5.9 %local_pairs.1.kick_in = f32[16,8,128]{2,1,0:T(8,128)S(1)} custom-call(s32[592]{0:T(1024)S(1)} %plan.1.plan_ref, s32[16]{0:T(128)S(1)} %copy-done.7, f32[3,512,128]{2,1,0:T(8,128)S(1)} %copy-done.1, f32[512,128]{1,0:T(8,128)S(1)} %copy-done.4, f32[32,128]{1,0:T(8,128)S(1)} %get-tuple-element.26._), custom_call_target="tpu_custom_call" | custom-call | flops 10000000 | bytes 10000 | tf_op jit(solution)/shard_map/local_pairs/pallas_call | solution.py:324
  41.8 0.0 collective-permute-done.5.r1
  41.8 0.0 collective-permute-done.6.r2
  41.9 0.0 collective-permute-done.7.r3
  41.9 0.0 collective-permute-done.4.r0
  41.9 0.0 copy-done.2
  41.9 0.7 %leaving.1 = (f32[16,8,128]{2,1,0:T(8,128)S(1)}, f32[7,4,128]{2,1,0:T(4,128)S(1)}, f32[7,4,128]{2,1,0:T(4,128)S(1)}, f32[7,4,128]{2,1,0:T(4,128)S(1)}, f32[7,4,128]{2,1,0:T(4,128)S(1)}) custom-call(s32[592]{0:T(1024)S(1)} %plan.1.plan_ref, s32[16]{0:T(128)S(1)} %copy-done.7, s32[16]{0:T(128)S(1)} %copy-done.8, f32[3,512,128]{2,1,0:T(8,128)S(1)} %copy-done.1, ...), custom_call_target="tpu_custom_call" | custom-call | tf_op jit(solution)/shard_map/leaving/pallas_call | solution.py:335
  42.6 6.4 %collective-permute-start.8 = (f32[7,4,128]{2,1,0:T(4,128)S(1)}, f32[7,4,128]{2,1,0:T(4,128)S(1)}, u32[]{:S(2)}, u32[]{:S(2)}) collective-permute-start(f32[7,4,128]{2,1,0:T(4,128)S(1)} %get-tuple-element.33), channel_id=1, source_target_pairs={{0,126},{1,127},{2,0},{3,1},{4,2},{5,3},{6,4},{7,5},{8,6},{9,7},{1... | collective-permute-start | bytes 43016 | tf_op jit(solution)/shard_map/ppermute | solution.py:41
  49.0 2.2 %collective-permute-start.9 = (f32[7,4,128]{2,1,0:T(4,128)S(1)}, f32[7,4,128]{2,1,0:T(4,128)S(1)}, u32[]{:S(2)}, u32[]{:S(2)}) collective-permute-start(f32[7,4,128]{2,1,0:T(4,128)S(1)} %get-tuple-element.34), channel_id=1, source_target_pairs={{0,127},{1,0},{2,1},{3,2},{4,3},{5,4},{6,5},{7,6},{8,7},{9,8},{10,... | collective-permute-start | bytes 43016 | tf_op jit(solution)/shard_map/ppermute | solution.py:41
  51.3 0.0 collective-permute-start.10
  51.3 0.0 collective-permute-start.11
  51.3 11.1 %staying.1 = (f32[3,512,128]{2,1,0:T(8,128)}, f32[3,512,128]{2,1,0:T(8,128)}) custom-call(s32[592]{0:T(1024)S(1)} %plan.1.plan_ref, s32[16]{0:T(128)S(1)} %copy-done.7, f32[3,512,128]{2,1,0:T(8,128)S(1)} %copy-done.1, f32[3,512,128]{2,1,0:T(8,128)S(1)} %copy-done.2, f32[16,8,128]{2,1,0:T(8,128)S(1)} %get-tuple-element.30.kick_in, ...), custom_call_target="tpu_custom_call" | custom-call | flops 100000000 | bytes 10000 | tf_op jit(solution)/shard_map/staying/pallas_call | solution.py:345
  62.4 0.0 collective-permute-done.8
  62.4 0.0 collective-permute-done.9
  62.4 0.0 collective-permute-done.10
  62.4 0.0 collective-permute-done.11
  62.4 0.6 %pad_maximum_fusion = f32[7,16,128]{2,1,0:T(8,128)} fusion(f32[7,4,128]{2,1,0:T(4,128)S(1)} %collective-permute-done.11, f32[7,4,128]{2,1,0:T(4,128)S(1)} %collective-permute-done.10, f32[7,4,128]{2,1,0:T(4,128)S(1)} %collective-permute-done.9, f32[7,4,128]{2,1,0:T(4,128)S(1)} %collective-permute-done.8), kind=kLoop, calls=%fused_computation | loop fusion | flops 43008 | bytes 114688 | tf_op jit(solution)/shard_map/concatenate | solution.py:355
  (1 shorter events, 0.0 us)
Async XLA Ops:
  0.6 0.7 %copy-start.5 = (s32[16,16]{1,0:T(8,128)S(1)}, s32[16,16]{1,0:T(8,128)}, u32[]{:S(2)}) copy-start(s32[16,16]{1,0:T(8,128)} %owner_ref.1) | copy-start | bytes 3076
  1.3 0.7 %copy-start.6 = (s32[16,16]{1,0:T(8,128)S(1)}, s32[16,16]{1,0:T(8,128)}, u32[]{:S(2)}) copy-start(s32[16,16]{1,0:T(8,128)} %leaf_ref.1) | copy-start | bytes 3076
  3.5 11.1 %collective-permute-start = (s32[1,128]{1,0:T(1,128)S(1)}, s32[1,128]{1,0:T(1,128)S(1)}, u32[]{:S(2)}, u32[]{:S(2)}) collective-permute-start(s32[1,128]{1,0:T(1,128)S(1)} %get-tuple-element.22), channel_id=1, source_target_pairs={{0,126},{1,127},{2,0},{3,1},{4,2},{5,3},{6,4},{7,5},{8,6},{9,7},{1... | collective-permute-start | bytes 1544 | tf_op jit(solution)/shard_map/ppermute | solution.py:41
  12.8 3.0 %collective-permute-start.1 = (s32[1,128]{1,0:T(1,128)S(1)}, s32[1,128]{1,0:T(1,128)S(1)}, u32[]{:S(2)}, u32[]{:S(2)}) collective-permute-start(s32[1,128]{1,0:T(1,128)S(1)} %get-tuple-element.23), channel_id=1, source_target_pairs={{0,127},{1,0},{2,1},{3,2},{4,3},{5,4},{6,5},{7,6},{8,7},{9,8},{10,... | collective-permute-start | bytes 1544 | tf_op jit(solution)/shard_map/ppermute | solution.py:41
  13.8 2.0 %collective-permute-start.2 = (s32[1,128]{1,0:T(1,128)S(1)}, s32[1,128]{1,0:T(1,128)S(1)}, u32[]{:S(2)}, u32[]{:S(2)}) collective-permute-start(s32[1,128]{1,0:T(1,128)S(1)} %get-tuple-element.24), channel_id=1, source_target_pairs={{0,1},{1,2},{2,3},{3,4},{4,5},{5,6},{6,7},{7,8},{8,9},{9,10},{10,1... | collective-permute-start | bytes 1544 | tf_op jit(solution)/shard_map/ppermute | solution.py:41
  14.6 7.8 %collective-permute-start.3 = (s32[1,128]{1,0:T(1,128)S(1)}, s32[1,128]{1,0:T(1,128)S(1)}, u32[]{:S(2)}, u32[]{:S(2)}) collective-permute-start(s32[1,128]{1,0:T(1,128)S(1)} %get-tuple-element.25), channel_id=1, source_target_pairs={{0,2},{1,3},{2,4},{3,5},{4,6},{5,7},{6,8},{7,9},{8,10},{9,11},{10,... | collective-permute-start | bytes 1544 | tf_op jit(solution)/shard_map/ppermute | solution.py:41
  22.4 1.1 %copy-start = (f32[3,512,128]{2,1,0:T(8,128)S(1)}, f32[3,512,128]{2,1,0:T(8,128)}, u32[]{:S(2)}) copy-start(f32[3,512,128]{2,1,0:T(8,128)} %positions_ref.7) | copy-start | bytes 2359300
  23.5 0.9 %copy-start.3 = (f32[512,128]{1,0:T(8,128)S(1)}, f32[512,128]{1,0:T(8,128)}, u32[]{:S(2)}) copy-start(f32[512,128]{1,0:T(8,128)} %masses_ref.5) | copy-start | bytes 786436
  24.5 9.1 %copy-start.7 = (s32[16]{0:T(128)S(1)}, s32[16]{0:T(128)}, u32[]{:S(2)}) copy-start(s32[16]{0:T(128)} %active_ref.7) | copy-start | bytes 196
  24.5 9.1 %copy-start.8 = (s32[16]{0:T(128)S(1)}, s32[16]{0:T(128)}, u32[]{:S(2)}) copy-start(s32[16]{0:T(128)} %mig_ref.3) | copy-start | bytes 196
  24.5 11.5 %copy-start.1 = (f32[3,512,128]{2,1,0:T(8,128)S(1)}, f32[3,512,128]{2,1,0:T(8,128)}, u32[]{:S(2)}) copy-start(f32[3,512,128]{2,1,0:T(8,128)} %positions_ref.7) | copy-start | bytes 2359300
  24.5 11.5 %copy-start.4 = (f32[512,128]{1,0:T(8,128)S(1)}, f32[512,128]{1,0:T(8,128)}, u32[]{:S(2)}) copy-start(f32[512,128]{1,0:T(8,128)} %masses_ref.5) | copy-start | bytes 786436
  25.1 16.8 %copy-start.2 = (f32[3,512,128]{2,1,0:T(8,128)S(1)}, f32[3,512,128]{2,1,0:T(8,128)}, u32[]{:S(2)}) copy-start(f32[3,512,128]{2,1,0:T(8,128)} %velocities_ref.3) | copy-start | bytes 2359300
  25.1 16.7 %collective-permute-start.5 = (f32[32,128]{1,0:T(8,128)S(1)}, f32[32,128]{1,0:T(8,128)S(1)}, u32[]{:S(2)}, u32[]{:S(2)}) collective-permute-start(f32[32,128]{1,0:T(8,128)S(1)} %get-tuple-element.27), channel_id=1, source_target_pairs={{0,1},{1,2},{2,3},{3,4},{4,5},{5,6},{6,7},{7,8},{8,9},{9,10},{10,1... | collective-permute-start | bytes 49160 | tf_op jit(solution)/shard_map/ppermute | solution.py:41
  25.2 16.6 %collective-permute-start.6 = (f32[32,128]{1,0:T(8,128)S(1)}, f32[32,128]{1,0:T(8,128)S(1)}, u32[]{:S(2)}, u32[]{:S(2)}) collective-permute-start(f32[32,128]{1,0:T(8,128)S(1)} %get-tuple-element.28), channel_id=1, source_target_pairs={{0,127},{1,0},{2,1},{3,2},{4,3},{5,4},{6,5},{7,6},{8,7},{9,8},{10,... | collective-permute-start | bytes 49160 | tf_op jit(solution)/shard_map/ppermute | solution.py:41
  26.2 15.7 %collective-permute-start.7 = (f32[32,128]{1,0:T(8,128)S(1)}, f32[32,128]{1,0:T(8,128)S(1)}, u32[]{:S(2)}, u32[]{:S(2)}) collective-permute-start(f32[32,128]{1,0:T(8,128)S(1)} %get-tuple-element.29), channel_id=1, source_target_pairs={{0,126},{1,127},{2,0},{3,1},{4,2},{5,3},{6,4},{7,5},{8,6},{9,7},{1... | collective-permute-start | bytes 49160 | tf_op jit(solution)/shard_map/ppermute | solution.py:41
  32.9 9.0 %collective-permute-start.4 = (f32[32,128]{1,0:T(8,128)S(1)}, f32[32,128]{1,0:T(8,128)S(1)}, u32[]{:S(2)}, u32[]{:S(2)}) collective-permute-start(f32[32,128]{1,0:T(8,128)S(1)} %get-tuple-element.26._), channel_id=1, source_target_pairs={{0,2},{1,3},{2,4},{3,5},{4,6},{5,7},{6,8},{7,9},{8,10},{9,11},{10,... | collective-permute-start | bytes 49160 | tf_op jit(solution)/shard_map/ppermute | solution.py:41
  42.6 19.7 %collective-permute-start.8 = (f32[7,4,128]{2,1,0:T(4,128)S(1)}, f32[7,4,128]{2,1,0:T(4,128)S(1)}, u32[]{:S(2)}, u32[]{:S(2)}) collective-permute-start(f32[7,4,128]{2,1,0:T(4,128)S(1)} %get-tuple-element.33), channel_id=1, source_target_pairs={{0,126},{1,127},{2,0},{3,1},{4,2},{5,3},{6,4},{7,5},{8,6},{9,7},{1... | collective-permute-start | bytes 43016 | tf_op jit(solution)/shard_map/ppermute | solution.py:41
  49.0 13.3 %collective-permute-start.9 = (f32[7,4,128]{2,1,0:T(4,128)S(1)}, f32[7,4,128]{2,1,0:T(4,128)S(1)}, u32[]{:S(2)}, u32[]{:S(2)}) collective-permute-start(f32[7,4,128]{2,1,0:T(4,128)S(1)} %get-tuple-element.34), channel_id=1, source_target_pairs={{0,127},{1,0},{2,1},{3,2},{4,3},{5,4},{6,5},{7,6},{8,7},{9,8},{10,... | collective-permute-start | bytes 43016 | tf_op jit(solution)/shard_map/ppermute | solution.py:41
  51.3 11.1 %collective-permute-start.10 = (f32[7,4,128]{2,1,0:T(4,128)S(1)}, f32[7,4,128]{2,1,0:T(4,128)S(1)}, u32[]{:S(2)}, u32[]{:S(2)}) collective-permute-start(f32[7,4,128]{2,1,0:T(4,128)S(1)} %get-tuple-element.35), channel_id=1, source_target_pairs={{0,1},{1,2},{2,3},{3,4},{4,5},{5,6},{6,7},{7,8},{8,9},{9,10},{10,1... | collective-permute-start | bytes 43016 | tf_op jit(solution)/shard_map/ppermute | solution.py:41
  51.3 11.1 %collective-permute-start.11 = (f32[7,4,128]{2,1,0:T(4,128)S(1)}, f32[7,4,128]{2,1,0:T(4,128)S(1)}, u32[]{:S(2)}, u32[]{:S(2)}) collective-permute-start(f32[7,4,128]{2,1,0:T(4,128)S(1)} %get-tuple-element.36), channel_id=1, source_target_pairs={{0,2},{1,3},{2,4},{3,5},{4,6},{5,7},{6,8},{7,9},{8,10},{9,11},{10,... | collective-permute-start | bytes 43016 | tf_op jit(solution)/shard_map/ppermute | solution.py:41

commit v2 on v0

v2 whole, which is shorter than its diff:
```python
import functools
import math

import jax
import jax.numpy as jnp
from jax import lax
from jax.experimental import pallas as pl
from jax.experimental.pallas import tpu as pltpu
from jax.sharding import PartitionSpec as P

REACH = 2
SLOTS = 4
IMPORT = 8
ACT = 16
PARTNERS = 16
LANES = 128
SIDES = 2 * REACH
IMPORTS = SIDES * IMPORT
BIG = 1 << 20
OFFSETS = [o for o in range(-REACH, REACH + 1) if o != 0]

soften = 0.02
EPS = 4.0 * soften * soften
NEG_LOG2E = -math.log2(math.e)
TWO_OVER_ROOT_PI = 2.0 / math.sqrt(math.pi)

F32, BF16, I32 = jnp.float32, jnp.bfloat16, jnp.int32

CHUNK = 8
AHEAD = 2 * CHUNK
COARSE, ROWS = 16, 48
REMOTE, LOCAL, N_REMOTE, N_LOCAL, PLAN = 0, 304, 608, 609, 616
SLOT_BIT, LEAF_BIT, PLACE_BIT = 22, 13, 5

VMEM = pl.BlockSpec(memory_space=pltpu.VMEM)
SMEM = pl.BlockSpec(memory_space=pltpu.SMEM)
ANY = pl.BlockSpec(memory_space=pl.ANY)


def params(mib):
    return pltpu.CompilerParams(vmem_limit_bytes=mib << 20)


def shifted(shard, by):
    length = lax.axis_size("dom")
    return lax.ppermute(shard, "dom", [(i, (i + by) % length) for i in range(length)])


def request_kernel(domains, me_ref, owner_ref, leaf_ref, *outs):
    requests, map_ref, mult_ref = outs[:SIDES], outs[SIDES], outs[SIDES + 1]
    leaf = leaf_ref[...]
    relative = owner_ref[...] - me_ref[0] + REACH
    relative = jnp.where(relative < 0, relative + domains, relative)
    relative = jnp.where(relative >= domains, relative - domains, relative)
    lane = lax.broadcasted_iota(I32, (1, LANES), 1)
    place = IMPORTS + leaf
    for side, offset in enumerate(OFFSETS):
        mine = relative == offset + REACH
        key = jnp.where(mine, leaf, BIG)
        rank = jnp.zeros_like(leaf)
        row = jnp.zeros((1, LANES), I32)
        for k in range(IMPORT):
            least = jnp.min(jnp.min(key, axis=0, keepdims=True), axis=1, keepdims=True)
            row = jnp.where(lane == k, jnp.broadcast_to(least, row.shape), row)
            here = key == least
            rank = jnp.where(here, k, rank)
            key = jnp.where(here, BIG, key)
        requests[side][...] = jnp.minimum(row, 511)
        place = jnp.where(mine, side * IMPORT + rank, place)
    map_ref[...] = place
    column = lax.broadcasted_iota(I32, place.shape, 1)
    times = jnp.zeros_like(place)
    earlier = jnp.zeros_like(place)
    for k in range(PARTNERS):
        same = (place == place[:, k : k + 1]).astype(I32)
        times = times + same
        earlier = jnp.where(column > k, earlier + same, earlier)
    mult_ref[...] = jnp.where(earlier > 0, 0, times)


def plan_kernel(map_ref, mult_ref, count_ref, plan_ref):
    def one_slot(a, sizes):
        n_remote, n_local = sizes
        for k in range(PARTNERS):
            place, times = map_ref[a, k], mult_ref[a, k]
            word = (a << SLOT_BIT) + times
            plan_ref[REMOTE + AHEAD + n_remote] = word + (place << PLACE_BIT)
            plan_ref[LOCAL + AHEAD + n_local] = word + ((place - IMPORTS) << LEAF_BIT) + (n_local << PLACE_BIT)
            counts = jnp.where(times > 0, 1, 0)
            remote = jnp.where(place < IMPORTS, counts, 0)
            n_remote, n_local = n_remote + remote, n_local + counts - remote
        return n_remote, n_local

    n_remote, n_local = lax.fori_loop(0, count_ref[0], one_slot, (jnp.int32(0), jnp.int32(0)))
    for i in range(AHEAD):
        plan_ref[REMOTE + i] = 0
        plan_ref[LOCAL + i] = 0
    for i in range(3 * CHUNK):
        plan_ref[REMOTE + AHEAD + n_remote + i] = 0
        plan_ref[LOCAL + AHEAD + n_local + i] = 0
    plan_ref[N_REMOTE] = n_remote
    plan_ref[N_LOCAL] = n_local


def reply_kernel(r0, r1, r2, r3, _, positions_ref, masses_ref, o0, o1, o2, o3):
    for request, out in ((r0, o0), (r1, o1), (r2, o2), (r3, o3)):
        for k in range(IMPORT):
            at = pl.ds(request[0, k], 1)
            for c in range(3):
                out[8 * c + k : 8 * c + k + 1, :] = 2.0 * positions_ref[c, at, :]
            out[24 + k : 25 + k, :] = masses_ref[at, :]


def pieces(v):
    a = v.astype(BF16).astype(F32)
    b = (v - a).astype(BF16).astype(F32)
    return a, b, v - a - b


def split_rows(xs):
    h = [jnp.floor(x * 128.0 + 0.5) * (1.0 / 128.0) for x in xs]
    l = [x - y for x, y in zip(xs, h)]
    l1 = [v.astype(BF16).astype(F32) for v in l]
    l2 = [v - w for v, w in zip(l, l1)]
    coarse = h[0] * h[0] + h[1] * h[1] + h[2] * h[2]
    fine = sum(b * (2.0 * a + b) for a, b in zip(h, l))
    return h, l1, l2, coarse, fine


def times_minus_two(rows):
    return [-2.0 * r for r in rows]


def source_rows(xs):
    h, l1, l2, coarse, fine = split_rows(xs)
    one, none = jnp.ones_like(coarse), [None]
    first = times_minus_two(h) + [*pieces(coarse), one, one, one] + none * 7
    return first + [*h, *h, *l1, *l2, *l1, *l1, *l2, *l2, *pieces(fine), one, one, one] + none * 2


def target_rows(xs):
    h, l1, l2, coarse, fine = split_rows(xs)
    one, none = jnp.ones_like(coarse), [None]
    first = h + [one, one, one, *pieces(coarse)] + none * 7
    n1, n2, nh = times_minus_two(l1), times_minus_two(l2), times_minus_two(h)
    return first + [*n1, *n2, *nh, *nh, *n1, *n2, *n1, *n2, one, one, one, *pieces(fine + EPS)] + none * 2


def by_leaf(stage, rows, start=0):
    for r, row in enumerate(rows):
        stage[pl.ds(start + r, 8, stride=len(rows)), :] = jnp.zeros((8, LANES), F32) if row is None else row


def set_sources(first, xs, m, stage, sources, blocks):
    by_leaf(stage, source_rows(xs))
    pad = jnp.zeros((LANES - ROWS, LANES), F32)
    for k in range(8):
        wide = jnp.concatenate([stage[ROWS * k : ROWS * (k + 1), :], pad], axis=0)
        sources[first + k] = jnp.transpose(wide)[:, :ROWS].astype(BF16)
    rows = [*xs, jnp.ones_like(m), m] + [None] * 3
    by_leaf(blocks, rows, start=8 * first)


def run_list(plan_ref, base, n, targets, centers, sources, blocks, sums, square, split):
    square[...] = jnp.ones_like(square)
    split[...] = jnp.zeros_like(split)

    def fields(word):
        return lax.shift_right_logical(word, SLOT_BIT), lax.shift_right_logical(word, PLACE_BIT) & 255

    @pl.loop(0, lax.shift_right_logical(n + CHUNK - 1, 3) + 2)
    def _(q):
        start = base + q * CHUNK
        for t in range(CHUNK):
            word = plan_ref[start + t]
            slot, place = fields(word)
            block = blocks[pl.ds(pl.multiple_of(8 * place, 8), 8), :]
            mass = block[4:5] * (word & 31).astype(F32)
            a, b, c = pieces((block - centers[slot]) * mass)
            weights = jnp.concatenate([a, b, c, jnp.zeros_like(c)], axis=0).astype(BF16)
            out = jnp.dot(jnp.concatenate([weights, weights], axis=1), split[t], preferred_element_type=F32)
            sums[slot] += out[0:8] + out[8:16] + out[16:24]
        for t in range(CHUNK):
            sq = square[t]
            inverse = lax.rsqrt(sq)
            gauss = TWO_OVER_ROOT_PI * jnp.exp2(sq * NEG_LOG2E)
            law = ((1.0 - lax.erf(sq * inverse)) * inverse + gauss) * (inverse * inverse)
            high = law.astype(BF16)
            split[t, :LANES] = high
            split[t, LANES:] = (law - high.astype(F32)).astype(BF16)
        for t in range(CHUNK):
            slot, place = fields(plan_ref[start + AHEAD + t])
            square[t] = jnp.dot(
                sources[place, :, :COARSE], targets[slot, :COARSE], preferred_element_type=F32
            ) + jnp.dot(sources[place, :, COARSE:], targets[slot, COARSE:], preferred_element_type=F32)


def local_kernel(plan_ref, active_ref, positions_ref, masses_ref, _, sums, targets, centers,
                 held, stage, sources, blocks, square, split):
    for a in range(ACT):
        at = pl.ds(active_ref[a], 1)
        for c in range(3):
            held[16 * c + a : 16 * c + a + 1, :] = 2.0 * positions_ref[c, at, :]
    for g in range(ACT // 8):
        xs = [held[16 * c + 8 * g : 16 * c + 8 * g + 8, :] for c in range(3)]
        by_leaf(stage, target_rows(xs))
        for k in range(8):
            targets[8 * g + k] = stage[ROWS * k : ROWS * (k + 1), :].astype(BF16)
        means = [jnp.broadcast_to(jnp.mean(x, axis=1, keepdims=True), x.shape) for x in xs]
        by_leaf(stage, means + [None] * 5)
        for k in range(8):
            centers[8 * g + k] = stage[8 * k : 8 * k + 8, :]
    sums[...] = jnp.zeros_like(sums)
    n = plan_ref[N_LOCAL]

    @pl.when(n > 0)
    def _():
        @pl.loop(0, lax.shift_right_logical(n + 7, 3))
        def _(g):
            for k in range(8):
                word = plan_ref[LOCAL + AHEAD + 8 * g + k]
                at = pl.ds(lax.shift_right_logical(word, LEAF_BIT) & 511, 1)
                for c in range(3):
                    held[8 * c + k : 8 * c + k + 1, :] = 2.0 * positions_ref[c, at, :]
                held[24 + k : 25 + k, :] = masses_ref[at, :]
            xs = [held[8 * c : 8 * c + 8, :] for c in range(3)]
            set_sources(pl.multiple_of(8 * g, 8), xs, held[24:32, :], stage, sources, blocks)

        run_list(plan_ref, LOCAL, n, targets, centers, sources, blocks, sums, square, split)


def remote_kernel(plan_ref, active_ref, count_ref, mig_ref, positions_ref, velocities_ref, masses_ref,
                  sums_in, targets, centers, r0, r1, r2, r3, new_positions, new_velocities, b0, b1, b2, b3,
                  stage, sources, blocks, sums, square, split):
    for side, received in enumerate((r0, r1, r2, r3)):
        xs = [received[8 * c : 8 * c + 8, :] for c in range(3)]
        set_sources(8 * side, xs, received[24:32, :], stage, sources, blocks)
    sums[...] = sums_in[...]
    run_list(plan_ref, REMOTE, plan_ref[N_REMOTE], targets, centers, sources, blocks, sums, square, split)
    new_velocities[...] = velocities_ref[...]
    new_positions[...] = positions_ref[...] + 0.25 * velocities_ref[...]

    @pl.loop(0, count_ref[0])
    def _(a):
        at = pl.ds(active_ref[a], 1)
        total, center = sums[a], centers[a]
        for c in range(3):
            x = positions_ref[c, at, :]
            v = velocities_ref[c, at, :] + (total[c : c + 1] - (2.0 * x - center[c : c + 1]) * total[3:4])
            new_velocities[c, at, :] = v
            new_positions[c, at, :] = x + 0.25 * v

    for side, block in enumerate((b0, b1, b2, b3)):
        for k in range(SLOTS):
            leaf = mig_ref[side * SLOTS + k]
            at = pl.ds(jnp.maximum(leaf, 0), 1)
            held = jnp.full((1, LANES), jnp.where(leaf >= 0, 1, 0), I32) > 0
            for c in range(3):
                block[c, k : k + 1, :] = jnp.where(held, new_positions[c, at, :], 0.0)
                block[3 + c, k : k + 1, :] = jnp.where(held, new_velocities[c, at, :], 0.0)
            block[6, k : k + 1, :] = jnp.where(held, masses_ref[at, :], 0.0)


def shape(*dims, dtype=F32):
    return jax.ShapeDtypeStruct(dims, dtype)


def per_device(positions, velocities, masses, active_leaves, active_count, partner_owner, partner_leaf, mig_leaf):
    leaves = positions.shape[1]
    domains = lax.axis_size("dom")
    me = lax.axis_index("dom").astype(I32).reshape(1)
    *requests, place, times = pl.pallas_call(
        functools.partial(request_kernel, domains),
        out_shape=[shape(1, LANES, dtype=I32)] * SIDES + [shape(ACT, PARTNERS, dtype=I32)] * 2,
        in_specs=[SMEM, VMEM, VMEM],
        out_specs=[VMEM] * (SIDES + 2),
        compiler_params=params(4),
        name="requests",
    )(me, partner_owner, partner_leaf)
    asked = [shifted(r, o) for r, o in zip(requests, OFFSETS)]
    plan = pl.pallas_call(
        plan_kernel,
        out_shape=shape(PLAN, dtype=I32),
        in_specs=[SMEM] * 3,
        out_specs=SMEM,
        compiler_params=params(4),
        cost_estimate=pl.CostEstimate(flops=10_000_000, bytes_accessed=10_000, transcendentals=0),
        name="plan",
    )(place, times, active_count)
    replies = pl.pallas_call(
        reply_kernel,
        out_shape=[shape(4 * IMPORT, LANES)] * SIDES,
        in_specs=[SMEM] * SIDES + [ANY] + [VMEM] * 2,
        out_specs=[VMEM] * SIDES,
        compiler_params=params(4),
        name="replies",
    )(*asked, plan, positions, masses)
    received = [shifted(r, -o) for r, o in zip(replies, OFFSETS)]

    def tables(n):
        return [
            pltpu.VMEM((8 * ROWS, LANES), F32),
            pltpu.VMEM((n, LANES, ROWS), BF16),
            pltpu.VMEM((8 * n, LANES), F32),
        ]

    chunks = [pltpu.VMEM((CHUNK, LANES, LANES), F32), pltpu.VMEM((CHUNK, 2 * LANES, LANES), BF16)]
    sums = shape(ACT, 8, LANES)
    sums, targets, centers = pl.pallas_call(
        local_kernel,
        out_shape=[sums, shape(ACT, ROWS, LANES, dtype=BF16), sums],
        in_specs=[SMEM, SMEM, VMEM, VMEM, ANY],
        out_specs=[VMEM] * 3,
        scratch_shapes=[pltpu.VMEM((48, LANES), F32)] + tables(ACT * PARTNERS) + chunks,
        compiler_params=params(24),
        cost_estimate=pl.CostEstimate(flops=10_000_000, bytes_accessed=10_000, transcendentals=0),
        name="local_pairs",
    )(plan, active_leaves, positions, masses, replies[0])
    new_positions, new_velocities, *blocks = pl.pallas_call(
        remote_kernel,
        out_shape=[shape(3, leaves, LANES)] * 2 + [shape(7, SLOTS, LANES)] * SIDES,
        in_specs=[SMEM] * 4 + [VMEM] * (6 + SIDES),
        out_specs=[VMEM] * (2 + SIDES),
        scratch_shapes=tables(IMPORTS) + [pltpu.VMEM((ACT, 8, LANES), F32)] + chunks,
        compiler_params=params(16),
        cost_estimate=pl.CostEstimate(flops=100_000_000, bytes_accessed=10_000, transcendentals=0),
        name="remote_pairs",
    )(plan, active_leaves, active_count, mig_leaf, positions, velocities, masses, sums, targets, centers, *received)
    arrived = [shifted(b, o) for b, o in zip(blocks, OFFSETS)]
    arrived = jnp.concatenate(arrived, axis=1)
    return new_positions, new_velocities, arrived


def solution(mesh):
    return jax.shard_map(
        per_device,
        mesh=mesh,
        in_specs=(
            P(None, "dom", None),
            P(None, "dom", None),
            P("dom", None),
            P("dom"),
            P("dom"),
            P("dom", None),
            P("dom", None),
            P("dom"),
        ),
        out_specs=(P(None, "dom", None), P(None, "dom", None), P(None, "dom", None)),
        check_vma=False,
    )
```

time: 182 us -> 62.3 us (0.34)
  other arithmetic: 63.1 us -> 0.64 us
  loops' own time: 32.3 us -> 0 us
  local copies, waits for them, and re-layouts: 30.4 us -> 4.14 us
  waiting for transfers between devices: 31.6 us -> 18.2 us
  Pallas kernels: 0 us -> 13.4 us
  starting transfers between devices: 21.6 us -> 24.4 us
    mul x18 -> x0, other arithmetic: 45.6 us -> none  [the longest x16 45.5 us: pair_accel(): return jnp.sum(strength[None] * delta, axis=(1, 3))]
    another operation x1 -> x0, loops' own time: 32.3 us -> none  [per_device(): accel = lax.map(one_slot, (active_leaves, gathered))]
    ppermute x8 -> x12, waiting for transfers between devices: 31.6 us -> 18.2 us  [shifted(): lax.ppermute(shard, 'dom', [(i, (i + by) % length) for i in range(length)])]
    pallas_call x0 -> x5, Pallas kernels: none -> 13.4 us  [the longest x1 6.2 us: per_device(): pl.pallas_call(remote_kernel, out_shape=[shape(3, leaves, LANES)] * 2 + [...]
    dynamic_slice x32 -> x0, local copies, waits for them, and re-layouts: 9.57 us -> none  [per_device(): accel = lax.map(one_slot, (active_leaves, gathered))]
    reduce_sum x16 -> x0, other arithmetic: 7.35 us -> none  [pair_accel(): return jnp.sum(strength[None] * delta, axis=(1, 3))]
    sub x16 -> x0, other arithmetic: 6.53 us -> none  [pair_accel(): delta = source[:, :, None, :] - target[:, None, :, None]]
    gather x3 -> x0, local copies, waits for them, and re-layouts: 5.68 us -> none  [the longest x2 3.53 us: per_device(): gathered = jnp.moveaxis(buffer[:, lookup, :], 1, 0)]
  transfers between devices with their start and end apart: 8 -> 12, of which waited for: 5 -> 4; matrix products, arithmetic and copies ran while one was open for 4% -> 0% of each run, Pallas kernels for 0% -> 8%
where the time goes in v2:
time: 62.3 us; the launch traced here: 62.2 us
  starting transfers between devices  24.4 us (39%)
  waiting for transfers between devices  18.2 us (29%)
  Pallas kernels  13.4 us (22%)
  local copies, waits for them, and re-layouts  4.14 us (7%)
  between operations  1.41 us (2%)
  other arithmetic  0.64 us (1%)
    ppermute x12, starting transfers between devices, shifted(): lax.ppermute(shard, 'dom', [(i, (i + by) % length) for i in range(length)])  24.4 us
    ppermute x12, waiting for transfers between devices, shifted(): lax.ppermute(shard, 'dom', [(i, (i + by) % length) for i in range(length)])  18.2 us
    pallas_call x1, Pallas kernels, per_device(): pl.pallas_call(remote_kernel, out_shape=[shape(3, leaves, LANES)] * 2 + [...  6.2 us
    unnamed x18, local copies, waits for them, and re-layouts  4.14 us
    pallas_call x1, Pallas kernels, per_device(): pl.pallas_call(local_kernel, out_shape=[sums, shape(ACT, ROWS, LANES, dty...  3.14 us
    pallas_call x1, Pallas kernels, per_device(): pl.pallas_call(plan_kernel, out_shape=shape(PLAN, dtype=I32), in_specs=[S...  1.92 us
    pallas_call x1, Pallas kernels, per_device(): pl.pallas_call(functools.partial(request_kernel, domains), out_shape=[sha...  1.48 us
  transfers between devices with their start and end apart: 12, of which 4 were waited for; matrix products, arithmetic and copies ran while one was open for 0% of the time, Pallas kernels for 8%

profile of v2, /device:TPU:1, one launch (start us, length us, event | category | flops | bytes accessed | tf_op | source)
XLA Modules:
  0.0 62.2 jit_solution(9739506713579341454)
XLA Ops:
  0.6 0.0 copy-start.5
  0.6 0.7 %copy-done.5 = s32[16,16]{1,0:T(8,128)S(1)} copy-done((s32[16,16]{1,0:T(8,128)S(1)}, s32[16,16]{1,0:T(8,128)}, u32[]{:S(2)}) %copy-start.5) | copy-done | bytes 1048
  1.3 0.0 copy-start.6
  1.3 0.7 %copy-done.6 = s32[16,16]{1,0:T(8,128)S(1)} copy-done((s32[16,16]{1,0:T(8,128)S(1)}, s32[16,16]{1,0:T(8,128)}, u32[]{:S(2)}) %copy-start.6) | copy-done | bytes 1048
  2.0 1.5 %requests.1 = (s32[1,128]{1,0:T(1,128)S(1)}, s32[1,128]{1,0:T(1,128)S(1)}, s32[1,128]{1,0:T(1,128)S(1)}, s32[1,128]{1,0:T(1,128)S(1)}, s32[16,16]{1,0:T(8,128)S(1)}, /*index=5*/s32[16,16]{1,0:T(8,128)S(1)}) custom-call(s32[1]{0:T(128)} %bitcast.me_ref, s32[16,16]{1,0:T(8,128)S(1)} %copy-done.5, s32[16,16]{1,0:T(8,128)S(1)} %copy-done.6), custom_call_target="tpu_custom_call" | custom-call | tf_op jit(solution)/shard_map/requests/pallas_call | solution.py:272
  3.5 9.3 %collective-permute-start = (s32[1,128]{1,0:T(1,128)S(1)}, s32[1,128]{1,0:T(1,128)S(1)}, u32[]{:S(2)}, u32[]{:S(2)}) collective-permute-start(s32[1,128]{1,0:T(1,128)S(1)} %get-tuple-element.24), channel_id=1, source_target_pairs={{0,126},{1,127},{2,0},{3,1},{4,2},{5,3},{6,4},{7,5},{8,6},{9,7},{1... | collective-permute-start | bytes 1544 | tf_op jit(solution)/shard_map/ppermute | solution.py:46
  12.8 1.0 %collective-permute-start.1 = (s32[1,128]{1,0:T(1,128)S(1)}, s32[1,128]{1,0:T(1,128)S(1)}, u32[]{:S(2)}, u32[]{:S(2)}) collective-permute-start(s32[1,128]{1,0:T(1,128)S(1)} %get-tuple-element.25), channel_id=1, source_target_pairs={{0,127},{1,0},{2,1},{3,2},{4,3},{5,4},{6,5},{7,6},{8,7},{9,8},{10,... | collective-permute-start | bytes 1544 | tf_op jit(solution)/shard_map/ppermute | solution.py:46
  13.8 0.8 %collective-permute-start.2 = (s32[1,128]{1,0:T(1,128)S(1)}, s32[1,128]{1,0:T(1,128)S(1)}, u32[]{:S(2)}, u32[]{:S(2)}) collective-permute-start(s32[1,128]{1,0:T(1,128)S(1)} %get-tuple-element.26), channel_id=1, source_target_pairs={{0,1},{1,2},{2,3},{3,4},{4,5},{5,6},{6,7},{7,8},{8,9},{9,10},{10,1... | collective-permute-start | bytes 1544 | tf_op jit(solution)/shard_map/ppermute | solution.py:46
  14.6 0.0 collective-permute-start.3
  15.2 1.9 %plan.1._.plan_ref = s32[616]{0:T(1024)S(1)} custom-call(s32[16,16]{1,0:T(8,128)S(1)} %get-tuple-element.22.map_ref, s32[16,16]{1,0:T(8,128)S(1)} %get-tuple-element.23.mult_ref, s32[1]{0:T(128)S(6)} %copy.11.count_ref), custom_call_target="tpu_custom_call" | custom-call | flops 10000000 | bytes 10000 | tf_op jit(solution)/shard_map/plan/pallas_call | solution.py:281
  17.1 0.0 collective-permute-done.r0
  17.2 0.0 collective-permute-done.1.r1
  17.2 0.0 collective-permute-done.2.r2
  17.2 5.2 %collective-permute-done.3.r3 = s32[1,128]{1,0:T(1,128)S(1)} collective-permute-done((s32[1,128]{1,0:T(1,128)S(1)}, s32[1,128]{1,0:T(1,128)S(1)}, u32[]{:S(2)}, u32[]{:S(2)}) %collective-permute-start.3) | collective-permute-done | bytes 544 | tf_op jit(solution)/shard_map/ppermute | solution.py:46
  22.4 0.0 copy-start
  22.4 1.1 %copy-done = f32[3,512,128]{2,1,0:T(8,128)S(1)} copy-done((f32[3,512,128]{2,1,0:T(8,128)S(1)}, f32[3,512,128]{2,1,0:T(8,128)}, u32[]{:S(2)}) %copy-start) | copy-done | bytes 786456
  23.5 0.0 copy-start.2
  23.5 0.9 %copy-done.2 = f32[512,128]{1,0:T(8,128)S(1)} copy-done((f32[512,128]{1,0:T(8,128)S(1)}, f32[512,128]{1,0:T(8,128)}, u32[]{:S(2)}) %copy-start.2) | copy-done | bytes 262168
  24.5 0.0 copy-start.1
  24.5 0.0 copy-start.3
  24.5 0.0 copy-start.7
  24.5 0.6 %replies.1 = (f32[32,128]{1,0:T(8,128)S(1)}, f32[32,128]{1,0:T(8,128)S(1)}, f32[32,128]{1,0:T(8,128)S(1)}, f32[32,128]{1,0:T(8,128)S(1)}) custom-call(s32[1,128]{1,0:T(1,128)S(1)} %collective-permute-done.r0, s32[1,128]{1,0:T(1,128)S(1)} %collective-permute-done.1.r1, s32[1,128]{1,0:T(1,128)S(1)} %collective-permute-done.2.r2, ...), custom_call_target="tpu_custom_call" | custom-call | tf_op jit(solution)/shard_map/replies/pallas_call | solution.py:290
  25.1 0.0 copy-start.4
  25.1 0.1 collective-permute-start.5
  25.2 1.0 %collective-permute-start.6 = (f32[32,128]{1,0:T(8,128)S(1)}, f32[32,128]{1,0:T(8,128)S(1)}, u32[]{:S(2)}, u32[]{:S(2)}) collective-permute-start(f32[32,128]{1,0:T(8,128)S(1)} %get-tuple-element.33), channel_id=1, source_target_pairs={{0,127},{1,0},{2,1},{3,2},{4,3},{5,4},{6,5},{7,6},{8,7},{9,8},{10,... | collective-permute-start | bytes 49160 | tf_op jit(solution)/shard_map/ppermute | solution.py:46
  26.2 6.7 %collective-permute-start.7 = (f32[32,128]{1,0:T(8,128)S(1)}, f32[32,128]{1,0:T(8,128)S(1)}, u32[]{:S(2)}, u32[]{:S(2)}) collective-permute-start(f32[32,128]{1,0:T(8,128)S(1)} %get-tuple-element.34), channel_id=1, source_target_pairs={{0,126},{1,127},{2,0},{3,1},{4,2},{5,3},{6,4},{7,5},{8,6},{9,7},{1... | collective-permute-start | bytes 49160 | tf_op jit(solution)/shard_map/ppermute | solution.py:46
  32.9 0.0 collective-permute-start.4
  32.9 0.0 copy-done.1
  32.9 0.0 copy-done.3
  32.9 0.0 copy-done.7
  32.9 3.1 %local_pairs.1 = (f32[16,8,128]{2,1,0:T(8,128)S(1)}, bf16[16,48,128]{2,1,0:T(8,128)(2,1)S(1)}, f32[16,8,128]{2,1,0:T(8,128)S(1)}) custom-call(s32[616]{0:T(1024)S(1)} %plan.1._.plan_ref, s32[16]{0:T(128)S(1)} %copy-done.7, f32[3,512,128]{2,1,0:T(8,128)S(1)} %copy-done.1, f32[512,128]{1,0:T(8,128)S(1)} %copy-done.3, f32[32,128]{1,0:T(8,128)S(1)} %get-tuple-element.28._), custom_call_target="tpu_custom_call" | custom-call | flops 10000000 | bytes 10000 | tf_op jit(solution)/shard_map/local_pairs/pallas_call | solution.py:309
  36.1 0.0 collective-permute-done.5.r1
  36.1 0.0 collective-permute-done.6.r2
  36.1 0.0 collective-permute-done.7.r3
  36.1 4.8 %collective-permute-done.4.r0 = f32[32,128]{1,0:T(8,128)S(1)} collective-permute-done((f32[32,128]{1,0:T(8,128)S(1)}, f32[32,128]{1,0:T(8,128)S(1)}, u32[]{:S(2)}, u32[]{:S(2)}) %collective-permute-start.4) | collective-permute-done | bytes 16416 | tf_op jit(solution)/shard_map/ppermute | solution.py:46
  40.9 0.0 copy-start.8
  40.9 0.0 copy-done.4
  40.9 0.7 %copy-done.8 = s32[16]{0:T(128)S(1)} copy-done((s32[16]{0:T(128)S(1)}, s32[16]{0:T(128)}, u32[]{:S(2)}) %copy-start.8) | copy-done | bytes 88
  41.6 6.2 %remote_pairs.1 = (f32[3,512,128]{2,1,0:T(8,128)}, f32[3,512,128]{2,1,0:T(8,128)}, f32[7,4,128]{2,1,0:T(4,128)S(1)}, f32[7,4,128]{2,1,0:T(4,128)S(1)}, f32[7,4,1...) custom-call(s32[616]{0:T(1024)S(1)} %plan.1._.plan_ref, s32[16]{0:T(128)S(1)} %copy-done.7, s32[1]{0:T(128)S(6)} %copy.11.count_ref, ...), custom_call_target="tpu_custom_call" | custom-call | flops 100000000 | bytes 10000 | tf_op jit(solution)/shard_map/remote_pairs/pallas_call | solution.py:319
  47.8 2.1 %collective-permute-start.8 = (f32[7,4,128]{2,1,0:T(4,128)S(1)}, f32[7,4,128]{2,1,0:T(4,128)S(1)}, u32[]{:S(2)}, u32[]{:S(2)}) collective-permute-start(f32[7,4,128]{2,1,0:T(4,128)S(1)} %get-tuple-element.37), channel_id=1, source_target_pairs={{0,126},{1,127},{2,0},{3,1},{4,2},{5,3},{6,4},{7,5},{8,6},{9,7},{1... | collective-permute-start | bytes 43016 | tf_op jit(solution)/shard_map/ppermute | solution.py:46
  49.9 3.5 %collective-permute-start.9 = (f32[7,4,128]{2,1,0:T(4,128)S(1)}, f32[7,4,128]{2,1,0:T(4,128)S(1)}, u32[]{:S(2)}, u32[]{:S(2)}) collective-permute-start(f32[7,4,128]{2,1,0:T(4,128)S(1)} %get-tuple-element.38), channel_id=1, source_target_pairs={{0,127},{1,0},{2,1},{3,2},{4,3},{5,4},{6,5},{7,6},{8,7},{9,8},{10,... | collective-permute-start | bytes 43016 | tf_op jit(solution)/shard_map/ppermute | solution.py:46
  53.4 0.0 collective-permute-start.10
  53.4 0.0 collective-permute-start.11
  53.4 0.0 collective-permute-done.8
  53.4 1.6 %collective-permute-done.9 = f32[7,4,128]{2,1,0:T(4,128)S(1)} collective-permute-done((f32[7,4,128]{2,1,0:T(4,128)S(1)}, f32[7,4,128]{2,1,0:T(4,128)S(1)}, u32[]{:S(2)}, u32[]{:S(2)}) %collective-permute-start.9) | collective-permute-done | bytes 14368 | tf_op jit(solution)/shard_map/ppermute | solution.py:46
  54.9 0.0 collective-permute-done.10
  54.9 6.6 %collective-permute-done.11 = f32[7,4,128]{2,1,0:T(4,128)S(1)} collective-permute-done((f32[7,4,128]{2,1,0:T(4,128)S(1)}, f32[7,4,128]{2,1,0:T(4,128)S(1)}, u32[]{:S(2)}, u32[]{:S(2)}) %collective-permute-start.11) | collective-permute-done | bytes 14368 | tf_op jit(solution)/shard_map/ppermute | solution.py:46
  61.5 0.6 %pad_maximum_fusion = f32[7,16,128]{2,1,0:T(8,128)} fusion(f32[7,4,128]{2,1,0:T(4,128)S(1)} %collective-permute-done.11, f32[7,4,128]{2,1,0:T(4,128)S(1)} %collective-permute-done.10, f32[7,4,128]{2,1,0:T(4,128)S(1)} %collective-permute-done.9, f32[7,4,128]{2,1,0:T(4,128)S(1)} %collective-permute-done.8), kind=kLoop, calls=%fused_computation | loop fusion | flops 43008 | bytes 114688 | tf_op jit(solution)/shard_map/concatenate | solution.py:330
Async XLA Ops:
  0.6 0.7 %copy-start.5 = (s32[16,16]{1,0:T(8,128)S(1)}, s32[16,16]{1,0:T(8,128)}, u32[]{:S(2)}) copy-start(s32[16,16]{1,0:T(8,128)} %owner_ref.1) | copy-start | bytes 3076
  1.3 0.7 %copy-start.6 = (s32[16,16]{1,0:T(8,128)S(1)}, s32[16,16]{1,0:T(8,128)}, u32[]{:S(2)}) copy-start(s32[16,16]{1,0:T(8,128)} %leaf_ref.1) | copy-start | bytes 3076
  3.5 13.6 %collective-permute-start = (s32[1,128]{1,0:T(1,128)S(1)}, s32[1,128]{1,0:T(1,128)S(1)}, u32[]{:S(2)}, u32[]{:S(2)}) collective-permute-start(s32[1,128]{1,0:T(1,128)S(1)} %get-tuple-element.24), channel_id=1, source_target_pairs={{0,126},{1,127},{2,0},{3,1},{4,2},{5,3},{6,4},{7,5},{8,6},{9,7},{1... | collective-permute-start | bytes 1544 | tf_op jit(solution)/shard_map/ppermute | solution.py:46
  12.8 4.3 %collective-permute-start.1 = (s32[1,128]{1,0:T(1,128)S(1)}, s32[1,128]{1,0:T(1,128)S(1)}, u32[]{:S(2)}, u32[]{:S(2)}) collective-permute-start(s32[1,128]{1,0:T(1,128)S(1)} %get-tuple-element.25), channel_id=1, source_target_pairs={{0,127},{1,0},{2,1},{3,2},{4,3},{5,4},{6,5},{7,6},{8,7},{9,8},{10,... | collective-permute-start | bytes 1544 | tf_op jit(solution)/shard_map/ppermute | solution.py:46
  13.8 3.4 %collective-permute-start.2 = (s32[1,128]{1,0:T(1,128)S(1)}, s32[1,128]{1,0:T(1,128)S(1)}, u32[]{:S(2)}, u32[]{:S(2)}) collective-permute-start(s32[1,128]{1,0:T(1,128)S(1)} %get-tuple-element.26), channel_id=1, source_target_pairs={{0,1},{1,2},{2,3},{3,4},{4,5},{5,6},{6,7},{7,8},{8,9},{9,10},{10,1... | collective-permute-start | bytes 1544 | tf_op jit(solution)/shard_map/ppermute | solution.py:46
  14.6 7.8 %collective-permute-start.3 = (s32[1,128]{1,0:T(1,128)S(1)}, s32[1,128]{1,0:T(1,128)S(1)}, u32[]{:S(2)}, u32[]{:S(2)}) collective-permute-start(s32[1,128]{1,0:T(1,128)S(1)} %get-tuple-element.27), channel_id=1, source_target_pairs={{0,2},{1,3},{2,4},{3,5},{4,6},{5,7},{6,8},{7,9},{8,10},{9,11},{10,... | collective-permute-start | bytes 1544 | tf_op jit(solution)/shard_map/ppermute | solution.py:46
  22.4 1.1 %copy-start = (f32[3,512,128]{2,1,0:T(8,128)S(1)}, f32[3,512,128]{2,1,0:T(8,128)}, u32[]{:S(2)}) copy-start(f32[3,512,128]{2,1,0:T(8,128)} %positions_ref.5) | copy-start | bytes 2359300
  23.5 0.9 %copy-start.2 = (f32[512,128]{1,0:T(8,128)S(1)}, f32[512,128]{1,0:T(8,128)}, u32[]{:S(2)}) copy-start(f32[512,128]{1,0:T(8,128)} %masses_ref.5) | copy-start | bytes 786436
  24.5 8.4 %copy-start.1 = (f32[3,512,128]{2,1,0:T(8,128)S(1)}, f32[3,512,128]{2,1,0:T(8,128)}, u32[]{:S(2)}) copy-start(f32[3,512,128]{2,1,0:T(8,128)} %positions_ref.5) | copy-start | bytes 2359300
  24.5 8.4 %copy-start.3 = (f32[512,128]{1,0:T(8,128)S(1)}, f32[512,128]{1,0:T(8,128)}, u32[]{:S(2)}) copy-start(f32[512,128]{1,0:T(8,128)} %masses_ref.5) | copy-start | bytes 786436
  24.5 8.4 %copy-start.7 = (s32[16]{0:T(128)S(1)}, s32[16]{0:T(128)}, u32[]{:S(2)}) copy-start(s32[16]{0:T(128)} %active_ref.3) | copy-start | bytes 196
  25.1 15.8 %copy-start.4 = (f32[3,512,128]{2,1,0:T(8,128)S(1)}, f32[3,512,128]{2,1,0:T(8,128)}, u32[]{:S(2)}) copy-start(f32[3,512,128]{2,1,0:T(8,128)} %velocities_ref.1) | copy-start | bytes 2359300
  25.1 10.9 %collective-permute-start.5 = (f32[32,128]{1,0:T(8,128)S(1)}, f32[32,128]{1,0:T(8,128)S(1)}, u32[]{:S(2)}, u32[]{:S(2)}) collective-permute-start(f32[32,128]{1,0:T(8,128)S(1)} %get-tuple-element.32), channel_id=1, source_target_pairs={{0,1},{1,2},{2,3},{3,4},{4,5},{5,6},{6,7},{7,8},{8,9},{9,10},{10,1... | collective-permute-start | bytes 49160 | tf_op jit(solution)/shard_map/ppermute | solution.py:46
  25.2 10.9 %collective-permute-start.6 = (f32[32,128]{1,0:T(8,128)S(1)}, f32[32,128]{1,0:T(8,128)S(1)}, u32[]{:S(2)}, u32[]{:S(2)}) collective-permute-start(f32[32,128]{1,0:T(8,128)S(1)} %get-tuple-element.33), channel_id=1, source_target_pairs={{0,127},{1,0},{2,1},{3,2},{4,3},{5,4},{6,5},{7,6},{8,7},{9,8},{10,... | collective-permute-start | bytes 49160 | tf_op jit(solution)/shard_map/ppermute | solution.py:46
  26.2 9.9 %collective-permute-start.7 = (f32[32,128]{1,0:T(8,128)S(1)}, f32[32,128]{1,0:T(8,128)S(1)}, u32[]{:S(2)}, u32[]{:S(2)}) collective-permute-start(f32[32,128]{1,0:T(8,128)S(1)} %get-tuple-element.34), channel_id=1, source_target_pairs={{0,126},{1,127},{2,0},{3,1},{4,2},{5,3},{6,4},{7,5},{8,6},{9,7},{1... | collective-permute-start | bytes 49160 | tf_op jit(solution)/shard_map/ppermute | solution.py:46
  32.9 8.0 %collective-permute-start.4 = (f32[32,128]{1,0:T(8,128)S(1)}, f32[32,128]{1,0:T(8,128)S(1)}, u32[]{:S(2)}, u32[]{:S(2)}) collective-permute-start(f32[32,128]{1,0:T(8,128)S(1)} %get-tuple-element.28._), channel_id=1, source_target_pairs={{0,2},{1,3},{2,4},{3,5},{4,6},{5,7},{6,8},{7,9},{8,10},{9,11},{10,... | collective-permute-start | bytes 49160 | tf_op jit(solution)/shard_map/ppermute | solution.py:46
  40.9 0.7 %copy-start.8 = (s32[16]{0:T(128)S(1)}, s32[16]{0:T(128)}, u32[]{:S(2)}) copy-start(s32[16]{0:T(128)} %mig_ref.1) | copy-start | bytes 196
  47.8 5.6 %collective-permute-start.8 = (f32[7,4,128]{2,1,0:T(4,128)S(1)}, f32[7,4,128]{2,1,0:T(4,128)S(1)}, u32[]{:S(2)}, u32[]{:S(2)}) collective-permute-start(f32[7,4,128]{2,1,0:T(4,128)S(1)} %get-tuple-element.37), channel_id=1, source_target_pairs={{0,126},{1,127},{2,0},{3,1},{4,2},{5,3},{6,4},{7,5},{8,6},{9,7},{1... | collective-permute-start | bytes 43016 | tf_op jit(solution)/shard_map/ppermute | solution.py:46
  49.9 5.1 %collective-permute-start.9 = (f32[7,4,128]{2,1,0:T(4,128)S(1)}, f32[7,4,128]{2,1,0:T(4,128)S(1)}, u32[]{:S(2)}, u32[]{:S(2)}) collective-permute-start(f32[7,4,128]{2,1,0:T(4,128)S(1)} %get-tuple-element.38), channel_id=1, source_target_pairs={{0,127},{1,0},{2,1},{3,2},{4,3},{5,4},{6,5},{7,6},{8,7},{9,8},{10,... | collective-permute-start | bytes 43016 | tf_op jit(solution)/shard_map/ppermute | solution.py:46
  53.4 1.6 %collective-permute-start.10 = (f32[7,4,128]{2,1,0:T(4,128)S(1)}, f32[7,4,128]{2,1,0:T(4,128)S(1)}, u32[]{:S(2)}, u32[]{:S(2)}) collective-permute-start(f32[7,4,128]{2,1,0:T(4,128)S(1)} %get-tuple-element.39), channel_id=1, source_target_pairs={{0,1},{1,2},{2,3},{3,4},{4,5},{5,6},{6,7},{7,8},{8,9},{9,10},{10,1... | collective-permute-start | bytes 43016 | tf_op jit(solution)/shard_map/ppermute | solution.py:46
  53.4 8.2 %collective-permute-start.11 = (f32[7,4,128]{2,1,0:T(4,128)S(1)}, f32[7,4,128]{2,1,0:T(4,128)S(1)}, u32[]{:S(2)}, u32[]{:S(2)}) collective-permute-start(f32[7,4,128]{2,1,0:T(4,128)S(1)} %get-tuple-element.40), channel_id=1, source_target_pairs={{0,2},{1,3},{2,4},{3,5},{4,6},{5,7},{6,8},{7,9},{8,10},{9,11},{10,... | collective-permute-start | bytes 43016 | tf_op jit(solution)/shard_map/ppermute | solution.py:46

commit v3 on v2

--- a/solution.py
+++ b/solution.py
@@ -17,7 +17,6 @@
 SIDES = 2 * REACH
 IMPORTS = SIDES * IMPORT
 BIG = 1 << 20
-OFFSETS = [o for o in range(-REACH, REACH + 1) if o != 0]
 
 soften = 0.02
 EPS = 4.0 * soften * soften
@@ -29,32 +28,53 @@
 CHUNK = 8
 AHEAD = 2 * CHUNK
 COARSE, ROWS = 16, 48
-REMOTE, LOCAL, N_REMOTE, N_LOCAL, PLAN = 0, 304, 608, 609, 616
+LEAVING, STAYING, LOCAL, SIZES, LIVE, ACTIVE, MIG, FROM, PLAN = 0, 304, 608, 912, 915, 920, 936, 952, 968
 SLOT_BIT, LEAF_BIT, PLACE_BIT = 22, 13, 5
 
 VMEM = pl.BlockSpec(memory_space=pltpu.VMEM)
 SMEM = pl.BlockSpec(memory_space=pltpu.SMEM)
 ANY = pl.BlockSpec(memory_space=pl.ANY)
+HBM = pl.BlockSpec(memory_space=pltpu.HBM)
 
 
 def params(mib):
     return pltpu.CompilerParams(vmem_limit_bytes=mib << 20)
 
 
-def shifted(shard, by):
-    length = lax.axis_size("dom")
-    return lax.ppermute(shard, "dom", [(i, (i + by) % length) for i in range(length)])
-
-
-def request_kernel(domains, me_ref, owner_ref, leaf_ref, *outs):
-    requests, map_ref, mult_ref = outs[:SIDES], outs[SIDES], outs[SIDES + 1]
+def swapped(shard, partner):
+    return lax.ppermute(shard, "dom", [(i, partner(i) % lax.axis_size("dom")) for i in range(lax.axis_size("dom"))])
+
+
+PARTNERS_OF = (
+    lambda d: d + 2 if d & 2 else d - 2,
+    lambda d: d + 1 if d & 1 else d - 1,
+    lambda d: d ^ 2,
+    lambda d: d ^ 1,
+)
+
+
+def swap_offsets(me):
+    one, two = 1 - 2 * (me & 1), 2 - 2 * (me & 2)
+    return -two, -one, two, one
+
+
+def request_kernel(domains, me_ref, owner_hbm, leaf_hbm, *outs):
+    requests, (map_ref, mult_ref, owner_ref, leaf_ref, owner_sem, leaf_sem) = outs[:SIDES], outs[SIDES:]
+    copies = [
+        pltpu.make_async_copy(owner_hbm, owner_ref, owner_sem),
+        pltpu.make_async_copy(leaf_hbm, leaf_ref, leaf_sem),
+    ]
+    for copy in copies:
+        copy.start()
+    for copy in copies:
+        copy.wait()
     leaf = leaf_ref[...]
     relative = owner_ref[...] - me_ref[0] + REACH
     relative = jnp.where(relative < 0, relative + domains, relative)
     relative = jnp.where(relative >= domains, relative - domains, relative)
     lane = lax.broadcasted_iota(I32, (1, LANES), 1)
     place = IMPORTS + leaf
-    for side, offset in enumerate(OFFSETS):
+    for side, offset in enumerate(swap_offsets(me_ref[0])):
         mine = relative == offset + REACH
         key = jnp.where(mine, leaf, BIG)
         rank = jnp.zeros_like(leaf)
@@ -78,37 +98,65 @@
     mult_ref[...] = jnp.where(earlier > 0, 0, times)
 
 
-def plan_kernel(map_ref, mult_ref, count_ref, plan_ref):
-    def one_slot(a, sizes):
-        n_remote, n_local = sizes
+def plan_kernel(map_ref, mult_ref, count_ref, active_ref, mig_ref, positions_hbm, masses_hbm,
+                plan_ref, points, positions_sem, masses_sem):
+    copies = [
+        pltpu.make_async_copy(positions_hbm, points.at[:3], positions_sem),
+        pltpu.make_async_copy(masses_hbm, points.at[3], masses_sem),
+    ]
+    for copy in copies:
+        copy.start()
+    live = count_ref[0]
+    plan_ref[LIVE] = live
+    for n in range(SIDES * SLOTS):
+        plan_ref[MIG + n] = mig_ref[n]
+        plan_ref[FROM + n] = -1
+    for a in range(ACT):
+        plan_ref[ACTIVE + a] = active_ref[a]
+
+    def one_slot(a, ends):
+        leaving_end, staying_end, n_local = ends
+        leaf = active_ref[a]
+        hits = jnp.int32(0)
+        for n in range(SIDES * SLOTS):
+            hit = mig_ref[n] == leaf
+            plan_ref[FROM + n] = jnp.where(hit, a, plan_ref[FROM + n])
+            hits = hits + jnp.where(hit, 1, 0)
+        end = jnp.where(hits > 0, leaving_end, staying_end)
         for k in range(PARTNERS):
             place, times = map_ref[a, k], mult_ref[a, k]
             word = (a << SLOT_BIT) + times
-            plan_ref[REMOTE + AHEAD + n_remote] = word + (place << PLACE_BIT)
+            plan_ref[end] = word + (place << PLACE_BIT)
             plan_ref[LOCAL + AHEAD + n_local] = word + ((place - IMPORTS) << LEAF_BIT) + (n_local << PLACE_BIT)
             counts = jnp.where(times > 0, 1, 0)
             remote = jnp.where(place < IMPORTS, counts, 0)
-            n_remote, n_local = n_remote + remote, n_local + counts - remote
-        return n_remote, n_local
-
-    n_remote, n_local = lax.fori_loop(0, count_ref[0], one_slot, (jnp.int32(0), jnp.int32(0)))
+            end, n_local = end + remote, n_local + counts - remote
+        return jnp.where(hits > 0, end, leaving_end), jnp.where(hits > 0, staying_end, end), n_local
+
+    starts = (jnp.int32(LEAVING + AHEAD), jnp.int32(STAYING + AHEAD), jnp.int32(0))
+    leaving_end, staying_end, n_local = lax.fori_loop(0, live, one_slot, starts)
     for i in range(AHEAD):
-        plan_ref[REMOTE + i] = 0
+        plan_ref[LEAVING + i] = 0
+        plan_ref[STAYING + i] = 0
         plan_ref[LOCAL + i] = 0
     for i in range(3 * CHUNK):
-        plan_ref[REMOTE + AHEAD + n_remote + i] = 0
+        plan_ref[leaving_end + i] = 0
+        plan_ref[staying_end + i] = 0
         plan_ref[LOCAL + AHEAD + n_local + i] = 0
-    plan_ref[N_REMOTE] = n_remote
-    plan_ref[N_LOCAL] = n_local
-
-
-def reply_kernel(r0, r1, r2, r3, _, positions_ref, masses_ref, o0, o1, o2, o3):
+    plan_ref[SIZES] = leaving_end - (LEAVING + AHEAD)
+    plan_ref[SIZES + 1] = staying_end - (STAYING + AHEAD)
+    plan_ref[SIZES + 2] = n_local
+    for copy in copies:
+        copy.wait()
+
+
+def reply_kernel(r0, r1, r2, r3, _, points, o0, o1, o2, o3):
     for request, out in ((r0, o0), (r1, o1), (r2, o2), (r3, o3)):
         for k in range(IMPORT):
             at = pl.ds(request[0, k], 1)
             for c in range(3):
-                out[8 * c + k : 8 * c + k + 1, :] = 2.0 * positions_ref[c, at, :]
-            out[24 + k : 25 + k, :] = masses_ref[at, :]
+                out[8 * c + k : 8 * c + k + 1, :] = 2.0 * points[c, at, :]
+            out[24 + k : 25 + k, :] = points[3, at, :]
 
 
 def pieces(v):
@@ -195,12 +243,11 @@
             ) + jnp.dot(sources[place, :, COARSE:], targets[slot, COARSE:], preferred_element_type=F32)
 
 
-def local_kernel(plan_ref, active_ref, positions_ref, masses_ref, _, sums, targets, centers,
-                 held, stage, sources, blocks, square, split):
+def local_kernel(plan_ref, points, _, sums, targets, centers, held, stage, sources, blocks, square, split):
     for a in range(ACT):
-        at = pl.ds(active_ref[a], 1)
+        at = pl.ds(plan_ref[ACTIVE + a], 1)
         for c in range(3):
-            held[16 * c + a : 16 * c + a + 1, :] = 2.0 * positions_ref[c, at, :]
+            held[16 * c + a : 16 * c + a + 1, :] = 2.0 * points[c, at, :]
     for g in range(ACT // 8):
         xs = [held[16 * c + 8 * g : 16 * c + 8 * g + 8, :] for c in range(3)]
         by_leaf(stage, target_rows(xs))
@@ -211,7 +258,7 @@
         for k in range(8):
             centers[8 * g + k] = stage[8 * k : 8 * k + 8, :]
     sums[...] = jnp.zeros_like(sums)
-    n = plan_ref[N_LOCAL]
+    n = plan_ref[SIZES + 2]
 
     @pl.when(n > 0)
     def _():
@@ -221,44 +268,62 @@
                 word = plan_ref[LOCAL + AHEAD + 8 * g + k]
                 at = pl.ds(lax.shift_right_logical(word, LEAF_BIT) & 511, 1)
                 for c in range(3):
-                    held[8 * c + k : 8 * c + k + 1, :] = 2.0 * positions_ref[c, at, :]
-                held[24 + k : 25 + k, :] = masses_ref[at, :]
+                    held[8 * c + k : 8 * c + k + 1, :] = 2.0 * points[c, at, :]
+                held[24 + k : 25 + k, :] = points[3, at, :]
             xs = [held[8 * c : 8 * c + 8, :] for c in range(3)]
             set_sources(pl.multiple_of(8 * g, 8), xs, held[24:32, :], stage, sources, blocks)
 
         run_list(plan_ref, LOCAL, n, targets, centers, sources, blocks, sums, square, split)
 
 
-def remote_kernel(plan_ref, active_ref, count_ref, mig_ref, positions_ref, velocities_ref, masses_ref,
-                  sums_in, targets, centers, r0, r1, r2, r3, new_positions, new_velocities, b0, b1, b2, b3,
-                  stage, sources, blocks, sums, square, split):
+def kicked(x, v, total, center, c):
+    return v + (total[c : c + 1] - (2.0 * x - center[c : c + 1]) * total[3:4])
+
+
+def leaving_kernel(me_ref, plan_ref, points, velocities_ref, sums_in, targets, centers, r0, r1, r2, r3,
+                   sums, sources, blocks, b0, b1, b2, b3, stage, square, split):
     for side, received in enumerate((r0, r1, r2, r3)):
         xs = [received[8 * c : 8 * c + 8, :] for c in range(3)]
         set_sources(8 * side, xs, received[24:32, :], stage, sources, blocks)
     sums[...] = sums_in[...]
-    run_list(plan_ref, REMOTE, plan_ref[N_REMOTE], targets, centers, sources, blocks, sums, square, split)
+    n_leaving = plan_ref[SIZES]
+
+    @pl.when(n_leaving > 0)
+    def _():
+        run_list(plan_ref, LEAVING, n_leaving, targets, centers, sources, blocks, sums, square, split)
+
+    for offset, block in zip(swap_offsets(me_ref[0]), (b0, b1, b2, b3)):
+        number = SLOTS * (offset + jnp.where(offset < 0, REACH, REACH - 1))
+        for k in range(SLOTS):
+            leaf, a = plan_ref[MIG + number + k], plan_ref[FROM + number + k]
+            at = pl.ds(jnp.maximum(leaf, 0), 1)
+            held = jnp.full((1, LANES), jnp.where(leaf >= 0, 1, 0), I32) > 0
+            live = jnp.full((1, LANES), jnp.where(a >= 0, 1, 0), I32) > 0
+            total, center = sums[jnp.maximum(a, 0)], centers[jnp.maximum(a, 0)]
+            for c in range(3):
+                x, v = points[c, at, :], velocities_ref[c, at, :]
+                v = jnp.where(live, kicked(x, v, total, center, c), v)
+                block[c, k : k + 1, :] = jnp.where(held, x + 0.25 * v, 0.0)
+                block[3 + c, k : k + 1, :] = jnp.where(held, v, 0.0)
+            block[6, k : k + 1, :] = jnp.where(held, points[3, at, :], 0.0)
+
+
+def staying_kernel(plan_ref, points, velocities_ref, sums_in, targets, centers, sources, blocks,
+                   new_positions, new_velocities, sums, square, split):
+    sums[...] = sums_in[...]
     new_velocities[...] = velocities_ref[...]
-    new_positions[...] = positions_ref[...] + 0.25 * velocities_ref[...]
-
-    @pl.loop(0, count_ref[0])
+    new_positions[...] = points[:3] + 0.25 * velocities_ref[...]
+    run_list(plan_ref, STAYING, plan_ref[SIZES + 1], targets, centers, sources, blocks, sums, square, split)
+
+    @pl.loop(0, plan_ref[LIVE])
     def _(a):
-        at = pl.ds(active_ref[a], 1)
+        at = pl.ds(plan_ref[ACTIVE + a], 1)
         total, center = sums[a], centers[a]
         for c in range(3):
-            x = positions_ref[c, at, :]
-            v = velocities_ref[c, at, :] + (total[c : c + 1] - (2.0 * x - center[c : c + 1]) * total[3:4])
+            x = points[c, at, :]
+            v = kicked(x, velocities_ref[c, at, :], total, center, c)
             new_velocities[c, at, :] = v
             new_positions[c, at, :] = x + 0.25 * v
-
-    for side, block in enumerate((b0, b1, b2, b3)):
-        for k in range(SLOTS):
-            leaf = mig_ref[side * SLOTS + k]
-            at = pl.ds(jnp.maximum(leaf, 0), 1)
-            held = jnp.full((1, LANES), jnp.where(leaf >= 0, 1, 0), I32) > 0
-            for c in range(3):
-                block[c, k : k + 1, :] = jnp.where(held, new_positions[c, at, :], 0.0)
-                block[3 + c, k : k + 1, :] = jnp.where(held, new_velocities[c, at, :], 0.0)
-            block[6, k : k + 1, :] = jnp.where(held, masses_ref[at, :], 0.0)
 
 
 def shape(*dims, dtype=F32):
@@ -268,66 +333,85 @@
 def per_device(positions, velocities, masses, active_leaves, active_count, partner_owner, partner_leaf, mig_leaf):
     leaves = positions.shape[1]
     domains = lax.axis_size("dom")
-    me = lax.axis_index("dom").astype(I32).reshape(1)
+    me = lax.axis_index("dom").astype(I32)
+    dma = pltpu.SemaphoreType.DMA
+    entries = shape(ACT, PARTNERS, dtype=I32)
     *requests, place, times = pl.pallas_call(
         functools.partial(request_kernel, domains),
-        out_shape=[shape(1, LANES, dtype=I32)] * SIDES + [shape(ACT, PARTNERS, dtype=I32)] * 2,
-        in_specs=[SMEM, VMEM, VMEM],
+        out_shape=[shape(1, LANES, dtype=I32)] * SIDES + [entries] * 2,
+        in_specs=[SMEM, HBM, HBM],
         out_specs=[VMEM] * (SIDES + 2),
+        scratch_shapes=[pltpu.VMEM((ACT, PARTNERS), I32)] * 2 + [dma] * 2,
         compiler_params=params(4),
         name="requests",
-    )(me, partner_owner, partner_leaf)
-    asked = [shifted(r, o) for r, o in zip(requests, OFFSETS)]
-    plan = pl.pallas_call(
+    )(me.reshape(1), partner_owner, partner_leaf)
+    asked = [swapped(r, p) for r, p in zip(requests, PARTNERS_OF)]
+    plan, points = pl.pallas_call(
         plan_kernel,
-        out_shape=shape(PLAN, dtype=I32),
-        in_specs=[SMEM] * 3,
-        out_specs=SMEM,
+        out_shape=[shape(PLAN, dtype=I32), shape(4, leaves, LANES)],
+        in_specs=[SMEM] * 5 + [HBM] * 2,
+        out_specs=[SMEM, VMEM],
+        scratch_shapes=[dma] * 2,
         compiler_params=params(4),
         cost_estimate=pl.CostEstimate(flops=10_000_000, bytes_accessed=10_000, transcendentals=0),
         name="plan",
-    )(place, times, active_count)
+    )(place, times, active_count, active_leaves, mig_leaf, positions, masses)
     replies = pl.pallas_call(
         reply_kernel,
         out_shape=[shape(4 * IMPORT, LANES)] * SIDES,
-        in_specs=[SMEM] * SIDES + [ANY] + [VMEM] * 2,
+        in_specs=[SMEM] * SIDES + [ANY, VMEM],
         out_specs=[VMEM] * SIDES,
         compiler_params=params(4),
         name="replies",
-    )(*asked, plan, positions, masses)
-    received = [shifted(r, -o) for r, o in zip(replies, OFFSETS)]
-
-    def tables(n):
-        return [
-            pltpu.VMEM((8 * ROWS, LANES), F32),
-            pltpu.VMEM((n, LANES, ROWS), BF16),
-            pltpu.VMEM((8 * n, LANES), F32),
-        ]
-
+    )(*asked, plan, points)
+    received = [swapped(r, p) for r, p in zip(replies, PARTNERS_OF)]
+    stage = [pltpu.VMEM((8 * ROWS, LANES), F32)]
     chunks = [pltpu.VMEM((CHUNK, LANES, LANES), F32), pltpu.VMEM((CHUNK, 2 * LANES, LANES), BF16)]
-    sums = shape(ACT, 8, LANES)
+    slot_sums, all_own = shape(ACT, 8, LANES), ACT * PARTNERS
     sums, targets, centers = pl.pallas_call(
         local_kernel,
-        out_shape=[sums, shape(ACT, ROWS, LANES, dtype=BF16), sums],
-        in_specs=[SMEM, SMEM, VMEM, VMEM, ANY],
+        out_shape=[slot_sums, shape(ACT, ROWS, LANES, dtype=BF16), slot_sums],
+        in_specs=[SMEM, VMEM, ANY],
         out_specs=[VMEM] * 3,
-        scratch_shapes=[pltpu.VMEM((48, LANES), F32)] + tables(ACT * PARTNERS) + chunks,
+        scratch_shapes=[pltpu.VMEM((48, LANES), F32)]
+        + stage
+        + [pltpu.VMEM((all_own, LANES, ROWS), BF16), pltpu.VMEM((8 * all_own, LANES), F32)]
+        + chunks,
         compiler_params=params(24),
         cost_estimate=pl.CostEstimate(flops=10_000_000, bytes_accessed=10_000, transcendentals=0),
         name="local_pairs",
-    )(plan, active_leaves, positions, masses, replies[0])
-    new_positions, new_velocities, *blocks = pl.pallas_call(
-        remote_kernel,
-        out_shape=[shape(3, leaves, LANES)] * 2 + [shape(7, SLOTS, LANES)] * SIDES,
-        in_specs=[SMEM] * 4 + [VMEM] * (6 + SIDES),
-        out_specs=[VMEM] * (2 + SIDES),
-        scratch_shapes=tables(IMPORTS) + [pltpu.VMEM((ACT, 8, LANES), F32)] + chunks,
+    )(plan, points, replies[0])
+    sums, sources, tables, *blocks = pl.pallas_call(
+        leaving_kernel,
+        out_shape=[slot_sums, shape(IMPORTS, LANES, ROWS, dtype=BF16), shape(8 * IMPORTS, LANES)]
+        + [shape(7, SLOTS, LANES)] * SIDES,
+        in_specs=[SMEM] * 2 + [VMEM] * (5 + SIDES),
+        out_specs=[VMEM] * (3 + SIDES),
+        scratch_shapes=stage + chunks,
+        compiler_params=params(16),
+        name="leaving",
+    )(me.reshape(1), plan, points, velocities, sums, targets, centers, *received)
+    came = [swapped(b, p) for b, p in zip(blocks, PARTNERS_OF)]
+    new_positions, new_velocities = pl.pallas_call(
+        staying_kernel,
+        out_shape=[shape(3, leaves, LANES)] * 2,
+        in_specs=[SMEM] + [VMEM] * 7,
+        out_specs=[VMEM] * 2,
+        scratch_shapes=[pltpu.VMEM((ACT, 8, LANES), F32)] + chunks,
         compiler_params=params(16),
         cost_estimate=pl.CostEstimate(flops=100_000_000, bytes_accessed=10_000, transcendentals=0),
-        name="remote_pairs",
-    )(plan, active_leaves, active_count, mig_leaf, positions, velocities, masses, sums, targets, centers, *received)
-    arrived = [shifted(b, o) for b, o in zip(blocks, OFFSETS)]
-    arrived = jnp.concatenate(arrived, axis=1)
+        name="staying",
+    )(plan, points, velocities, sums, targets, centers, sources, tables)
+    first_two, even = (me & 2) == 0, (me & 1) == 0
+    arrived = jnp.concatenate(
+        [
+            jnp.where(first_two, came[2], came[0]),
+            jnp.where(even, came[3], came[1]),
+            jnp.where(even, came[1], came[3]),
+            jnp.where(first_two, came[0], came[2]),
+        ],
+        axis=1,
+    )
     return new_positions, new_velocities, arrived
 
 

time: 62.3 us -> 51.8 us (0.83)
  waiting for transfers between devices: 18.2 us -> 0.03 us
  starting transfers between devices: 24.4 us -> 30.8 us
  Pallas kernels: 13.4 us -> 14.4 us
    ppermute x12, waiting for transfers between devices: 18.2 us -> 0.03 us  [swapped(): lax.ppermute(shard, 'dom', [(i, partner(i) % lax.axis_size('dom')) for i...]
    ppermute x12, starting transfers between devices: 24.4 us -> 30.8 us  [swapped(): lax.ppermute(shard, 'dom', [(i, partner(i) % lax.axis_size('dom')) for i...]
    pallas_call x3 -> x4, Pallas kernels: 11.3 us -> 12.3 us  [the longest x1 5.63 us: per_device(): pl.pallas_call(staying_kernel, out_shape=[shape(3, leaves, LANES)] * 2, i...]
    unnamed x18 -> x14, local copies, waits for them, and re-layouts: 4.14 us -> 4.13 us
  transfers between devices with their start and end apart: 12 -> 12, of which waited for: 4 -> 0; matrix products, arithmetic and copies ran while one was open for 0% -> 0% of each run, Pallas kernels for 8% -> 21%
where the time goes in v3:
time: 51.8 us; the launch traced here: 51.5 us
  starting transfers between devices  30.8 us (59%)
  Pallas kernels  14.4 us (28%)
  local copies, waits for them, and re-layouts  4.13 us (8%)
  between operations  1.47 us (3%)
  other arithmetic  0.66 us (1%)
    ppermute x12, starting transfers between devices, swapped(): lax.ppermute(shard, 'dom', [(i, partner(i) % lax.axis_size('dom')) for i...  30.8 us
    pallas_call x1, Pallas kernels, per_device(): pl.pallas_call(staying_kernel, out_shape=[shape(3, leaves, LANES)] * 2, i...  5.63 us
    unnamed x14, local copies, waits for them, and re-layouts  4.13 us
    pallas_call x1, Pallas kernels, per_device(): pl.pallas_call(local_kernel, out_shape=[slot_sums, shape(ACT, ROWS, LANES...  3.17 us
    pallas_call x1, Pallas kernels, per_device(): pl.pallas_call(plan_kernel, out_shape=[shape(PLAN, dtype=I32), shape(4, l...  2.24 us
    pallas_call x1, Pallas kernels, per_device(): pl.pallas_call(functools.partial(request_kernel, domains), out_shape=[sha...  1.51 us
    pallas_call x1, Pallas kernels, per_device(): pl.pallas_call(leaving_kernel, out_shape=[slot_sums, shape(IMPORTS, LANES...  1.21 us
  transfers between devices with their start and end apart: 12, of which 0 were waited for; matrix products, arithmetic and copies ran while one was open for 0% of the time, Pallas kernels for 21%

profile of v3, /device:TPU:1, one launch (start us, length us, event | category | flops | bytes accessed | tf_op | source)
XLA Modules:
  0.0 51.5 jit_solution(438051104592282)
XLA Ops:
  0.6 0.0 copy-start.3
  0.6 0.7 %copy-done.3 = s32[16,16]{1,0:T(8,128)S(1)} copy-done((s32[16,16]{1,0:T(8,128)S(1)}, s32[16,16]{1,0:T(8,128)}, u32[]{:S(2)}) %copy-start.3) | copy-done | bytes 1048
  1.3 0.0 copy-start.4
  1.3 0.7 %copy-done.4 = s32[16,16]{1,0:T(8,128)S(1)} copy-done((s32[16,16]{1,0:T(8,128)S(1)}, s32[16,16]{1,0:T(8,128)}, u32[]{:S(2)}) %copy-start.4) | copy-done | bytes 1048
  2.0 1.5 %requests.1 = (s32[1,128]{1,0:T(1,128)S(1)}, s32[1,128]{1,0:T(1,128)S(1)}, s32[1,128]{1,0:T(1,128)S(1)}, s32[1,128]{1,0:T(1,128)S(1)}, s32[16,16]{1,0:T(8,128)S(1)}, /*index=5*/s32[16,16]{1,0:T(8,128)S(1)}) custom-call(s32[1]{0:T(128)} %bitcast.me_ref, s32[16,16]{1,0:T(8,128)S(1)} %copy-done.3, s32[16,16]{1,0:T(8,128)S(1)} %copy-done.4), custom_call_target="tpu_custom_call" | custom-call | tf_op jit(solution)/shard_map/requests/pallas_call | solution.py:339
  3.5 9.3 %collective-permute-start = (s32[1,128]{1,0:T(1,128)S(1)}, s32[1,128]{1,0:T(1,128)S(1)}, u32[]{:S(2)}, u32[]{:S(2)}) collective-permute-start(s32[1,128]{1,0:T(1,128)S(1)} %get-tuple-element.31), channel_id=1, source_target_pairs={{0,126},{1,127},{2,4},{3,5},{4,2},{5,3},{6,8},{7,9},{8,6},{9,7},{1... | collective-permute-start | bytes 1544 | tf_op jit(solution)/shard_map/ppermute | solution.py:45
  12.9 0.0 collective-permute-start.1
  12.9 0.0 collective-permute-start.2
  12.9 2.1 %collective-permute-start.3 = (s32[1,128]{1,0:T(1,128)S(1)}, s32[1,128]{1,0:T(1,128)S(1)}, u32[]{:S(2)}, u32[]{:S(2)}) collective-permute-start(s32[1,128]{1,0:T(1,128)S(1)} %get-tuple-element.34), channel_id=1, source_target_pairs={{0,1},{1,0},{2,3},{3,2},{4,5},{5,4},{6,7},{7,6},{8,9},{9,8},{10,11... | collective-permute-start | bytes 1544 | tf_op jit(solution)/shard_map/ppermute | solution.py:45
  15.7 0.0 copy-start.5
  15.7 0.0 copy-start.6
  15.7 0.6 %copy-done.5 = s32[16]{0:T(128)S(1)} copy-done((s32[16]{0:T(128)S(1)}, s32[16]{0:T(128)}, u32[]{:S(2)}) %copy-start.5) | copy-done | bytes 88
  16.3 0.0 copy-done.6
  16.3 0.0 copy-start.1
  16.3 1.1 %copy-done.1 = f32[3,512,128]{2,1,0:T(8,128)S(1)} copy-done((f32[3,512,128]{2,1,0:T(8,128)S(1)}, f32[3,512,128]{2,1,0:T(8,128)}, u32[]{:S(2)}) %copy-start.1) | copy-done | bytes 786456
  17.5 0.0 copy-start.2
  17.5 0.9 %copy-done.2 = f32[512,128]{1,0:T(8,128)S(1)} copy-done((f32[512,128]{1,0:T(8,128)S(1)}, f32[512,128]{1,0:T(8,128)}, u32[]{:S(2)}) %copy-start.2) | copy-done | bytes 262168
  18.4 2.2 %plan.1 = (s32[968]{0:T(1024)S(1)}, f32[4,512,128]{2,1,0:T(8,128)S(1)}) custom-call(s32[16,16]{1,0:T(8,128)S(1)} %get-tuple-element.27.map_ref, s32[16,16]{1,0:T(8,128)S(1)} %get-tuple-element.28.mult_ref, s32[1]{0:T(128)S(6)} %copy.11.count_ref, s32[16]{0:T(128)S(1)} %copy-done.5, s32[16]{0:T(128)S(1)} %copy-done.6, f32[3,512,128]{2,1,0:T(8,128)S(1)} %copy-done.1, ...), custom_call_target="tpu_custom_call" | custom-call | flops 10000000 | bytes 10000 | tf_op jit(solution)/shard_map/plan/pallas_call | solution.py:349
  20.7 0.0 collective-permute-done.r0
  20.7 0.0 collective-permute-done.1.r1
  20.7 0.0 collective-permute-done.2.r2
  20.7 0.0 collective-permute-done.3.r3
  20.7 0.6 %replies.1 = (f32[32,128]{1,0:T(8,128)S(1)}, f32[32,128]{1,0:T(8,128)S(1)}, f32[32,128]{1,0:T(8,128)S(1)}, f32[32,128]{1,0:T(8,128)S(1)}) custom-call(s32[1,128]{1,0:T(1,128)S(1)} %collective-permute-done.r0, s32[1,128]{1,0:T(1,128)S(1)} %collective-permute-done.1.r1, s32[1,128]{1,0:T(1,128)S(1)} %collective-permute-done.2.r2, ...), custom_call_target="tpu_custom_call" | custom-call | tf_op jit(solution)/shard_map/replies/pallas_call | solution.py:359
  21.3 0.0 copy-start
  21.4 6.0 %collective-permute-start.4 = (f32[32,128]{1,0:T(8,128)S(1)}, f32[32,128]{1,0:T(8,128)S(1)}, u32[]{:S(2)}, u32[]{:S(2)}) collective-permute-start(f32[32,128]{1,0:T(8,128)S(1)} %get-tuple-element.35._), channel_id=1, source_target_pairs={{0,126},{1,127},{2,4},{3,5},{4,2},{5,3},{6,8},{7,9},{8,6},{9,7},{1... | collective-permute-start | bytes 49160 | tf_op jit(solution)/shard_map/ppermute | solution.py:45
  27.3 0.0 collective-permute-start.5
  27.3 0.0 collective-permute-start.6
  27.3 2.1 %collective-permute-start.7 = (f32[32,128]{1,0:T(8,128)S(1)}, f32[32,128]{1,0:T(8,128)S(1)}, u32[]{:S(2)}, u32[]{:S(2)}) collective-permute-start(f32[32,128]{1,0:T(8,128)S(1)} %get-tuple-element.41), channel_id=1, source_target_pairs={{0,1},{1,0},{2,3},{3,2},{4,5},{5,4},{6,7},{7,6},{8,9},{9,8},{10,11... | collective-permute-start | bytes 49160 | tf_op jit(solution)/shard_map/ppermute | solution.py:45
  29.5 3.2 %local_pairs.1 = (f32[16,8,128]{2,1,0:T(8,128)S(1)}, bf16[16,48,128]{2,1,0:T(8,128)(2,1)S(1)}, f32[16,8,128]{2,1,0:T(8,128)S(1)}) custom-call(s32[968]{0:T(1024)S(1)} %get-tuple-element.29._.plan_ref, f32[4,512,128]{2,1,0:T(8,128)S(1)} %get-tuple-element.30.points, f32[32,128]{1,0:T(8,128)S(1)} %get-tuple-element.35._), custom_call_target="tpu_custom_call" | custom-call | flops 10000000 | bytes 10000 | tf_op jit(solution)/shard_map/local_pairs/pallas_call | solution.py:371
  32.7 0.0 collective-permute-done.4.r0
  32.7 0.0 collective-permute-done.5.r1
  32.7 0.0 collective-permute-done.6.r2
  32.7 0.0 collective-permute-done.7.r3
  32.7 0.0 copy-done
  32.7 1.2 %leaving.1 = (f32[16,8,128]{2,1,0:T(8,128)S(1)}, bf16[32,128,48]{2,1,0:T(8,128)(2,1)S(1)}, f32[256,128]{1,0:T(8,128)S(1)}, f32[7,4,128]{2,1,0:T(4,128)S(1)}, f32...) custom-call(s32[1]{0:T(128)} %bitcast.me_ref, s32[968]{0:T(1024)S(1)} %get-tuple-element.29._.plan_ref, ...), custom_call_target="tpu_custom_call" | custom-call | tf_op jit(solution)/shard_map/leaving/pallas_call | solution.py:384
  33.9 4.4 %collective-permute-start.10 = (f32[7,4,128]{2,1,0:T(4,128)S(1)}, f32[7,4,128]{2,1,0:T(4,128)S(1)}, u32[]{:S(2)}, u32[]{:S(2)}) collective-permute-start(f32[7,4,128]{2,1,0:T(4,128)S(1)} %get-tuple-element.49), channel_id=1, source_target_pairs={{0,1},{1,0},{2,3},{3,2},{4,5},{5,4},{6,7},{7,6},{8,9},{9,8},{10,11... | collective-permute-start | bytes 43016 | tf_op jit(solution)/shard_map/ppermute | solution.py:45
  38.3 0.0 collective-permute-start.11
  38.3 0.0 collective-permute-start.8
  38.3 6.9 %collective-permute-start.9 = (f32[7,4,128]{2,1,0:T(4,128)S(1)}, f32[7,4,128]{2,1,0:T(4,128)S(1)}, u32[]{:S(2)}, u32[]{:S(2)}) collective-permute-start(f32[7,4,128]{2,1,0:T(4,128)S(1)} %get-tuple-element.48), channel_id=1, source_target_pairs={{0,126},{1,127},{2,4},{3,5},{4,2},{5,3},{6,8},{7,9},{8,6},{9,7},{1... | collective-permute-start | bytes 43016 | tf_op jit(solution)/shard_map/ppermute | solution.py:45
  45.2 5.6 %staying.1 = (f32[3,512,128]{2,1,0:T(8,128)}, f32[3,512,128]{2,1,0:T(8,128)}) custom-call(s32[968]{0:T(1024)S(1)} %get-tuple-element.29._.plan_ref, f32[4,512,128]{2,1,0:T(8,128)S(1)} %get-tuple-element.30.points, f32[3,512,128]{2,1,0:T(8,128)S(1)} %copy-done, f32[16,8,128]{2,1,0:T(8,128)S(1)} %get-tuple-element.42.sums_in, ...), custom_call_target="tpu_custom_call" | custom-call | flops 100000000 | bytes 10000 | tf_op jit(solution)/shard_map/staying/pallas_call | solution.py:395
  50.8 0.0 collective-permute-done.10
  50.8 0.0 collective-permute-done.11
  50.8 0.0 collective-permute-done.8
  50.9 0.0 collective-permute-done.9
  50.9 0.6 %pad_maximum_fusion = f32[7,16,128]{2,1,0:T(8,128)} fusion(f32[7,4,128]{2,1,0:T(4,128)S(1)} %get-tuple-element.52, f32[7,4,128]{2,1,0:T(4,128)S(1)} %get-tuple-element.54, f32[7,4,128]{2,1,0:T(4,128)S(1)} %get-tuple-element.53, f32[7,4,128]{2,1,0:T(4,128)S(1)} %get-tuple-element.51), kind=kLoop, calls=%fused_computation | loop fusion | flops 43008 | bytes 114688 | tf_op jit(solution)/shard_map/concatenate | solution.py:406
  (2 shorter events, 0.0 us)
Async XLA Ops:
  0.6 0.7 %copy-start.3 = (s32[16,16]{1,0:T(8,128)S(1)}, s32[16,16]{1,0:T(8,128)}, u32[]{:S(2)}) copy-start(s32[16,16]{1,0:T(8,128)} %owner_hbm.1) | copy-start | bytes 3076
  1.3 0.7 %copy-start.4 = (s32[16,16]{1,0:T(8,128)S(1)}, s32[16,16]{1,0:T(8,128)}, u32[]{:S(2)}) copy-start(s32[16,16]{1,0:T(8,128)} %leaf_hbm.1) | copy-start | bytes 3076
  3.5 17.1 %collective-permute-start = (s32[1,128]{1,0:T(1,128)S(1)}, s32[1,128]{1,0:T(1,128)S(1)}, u32[]{:S(2)}, u32[]{:S(2)}) collective-permute-start(s32[1,128]{1,0:T(1,128)S(1)} %get-tuple-element.31), channel_id=1, source_target_pairs={{0,126},{1,127},{2,4},{3,5},{4,2},{5,3},{6,8},{7,9},{8,6},{9,7},{1... | collective-permute-start | bytes 1544 | tf_op jit(solution)/shard_map/ppermute | solution.py:45
  12.9 7.8 %collective-permute-start.1 = (s32[1,128]{1,0:T(1,128)S(1)}, s32[1,128]{1,0:T(1,128)S(1)}, u32[]{:S(2)}, u32[]{:S(2)}) collective-permute-start(s32[1,128]{1,0:T(1,128)S(1)} %get-tuple-element.32), channel_id=1, source_target_pairs={{0,127},{1,2},{2,1},{3,4},{4,3},{5,6},{6,5},{7,8},{8,7},{9,10},{10... | collective-permute-start | bytes 1544 | tf_op jit(solution)/shard_map/ppermute | solution.py:45
  12.9 7.8 %collective-permute-start.2 = (s32[1,128]{1,0:T(1,128)S(1)}, s32[1,128]{1,0:T(1,128)S(1)}, u32[]{:S(2)}, u32[]{:S(2)}) collective-permute-start(s32[1,128]{1,0:T(1,128)S(1)} %get-tuple-element.33), channel_id=1, source_target_pairs={{0,2},{1,3},{2,0},{3,1},{4,6},{5,7},{6,4},{7,5},{8,10},{9,11},{10,... | collective-permute-start | bytes 1544 | tf_op jit(solution)/shard_map/ppermute | solution.py:45
  12.9 7.8 %collective-permute-start.3 = (s32[1,128]{1,0:T(1,128)S(1)}, s32[1,128]{1,0:T(1,128)S(1)}, u32[]{:S(2)}, u32[]{:S(2)}) collective-permute-start(s32[1,128]{1,0:T(1,128)S(1)} %get-tuple-element.34), channel_id=1, source_target_pairs={{0,1},{1,0},{2,3},{3,2},{4,5},{5,4},{6,7},{7,6},{8,9},{9,8},{10,11... | collective-permute-start | bytes 1544 | tf_op jit(solution)/shard_map/ppermute | solution.py:45
  15.7 0.7 %copy-start.5 = (s32[16]{0:T(128)S(1)}, s32[16]{0:T(128)}, u32[]{:S(2)}) copy-start(s32[16]{0:T(128)} %active_ref.1) | copy-start | bytes 196
  15.7 0.7 %copy-start.6 = (s32[16]{0:T(128)S(1)}, s32[16]{0:T(128)}, u32[]{:S(2)}) copy-start(s32[16]{0:T(128)} %mig_ref.1) | copy-start | bytes 196
  16.3 1.1 %copy-start.1 = (f32[3,512,128]{2,1,0:T(8,128)S(1)}, f32[3,512,128]{2,1,0:T(8,128)}, u32[]{:S(2)}) copy-start(f32[3,512,128]{2,1,0:T(8,128)} %positions_hbm.1) | copy-start | bytes 2359300
  17.5 0.9 %copy-start.2 = (f32[512,128]{1,0:T(8,128)S(1)}, f32[512,128]{1,0:T(8,128)}, u32[]{:S(2)}) copy-start(f32[512,128]{1,0:T(8,128)} %masses_hbm.1) | copy-start | bytes 786436
  21.3 11.4 %copy-start = (f32[3,512,128]{2,1,0:T(8,128)S(1)}, f32[3,512,128]{2,1,0:T(8,128)}, u32[]{:S(2)}) copy-start(f32[3,512,128]{2,1,0:T(8,128)} %velocities_ref.3) | copy-start | bytes 2359300
  21.4 11.3 %collective-permute-start.4 = (f32[32,128]{1,0:T(8,128)S(1)}, f32[32,128]{1,0:T(8,128)S(1)}, u32[]{:S(2)}, u32[]{:S(2)}) collective-permute-start(f32[32,128]{1,0:T(8,128)S(1)} %get-tuple-element.35._), channel_id=1, source_target_pairs={{0,126},{1,127},{2,4},{3,5},{4,2},{5,3},{6,8},{7,9},{8,6},{9,7},{1... | collective-permute-start | bytes 49160 | tf_op jit(solution)/shard_map/ppermute | solution.py:45
  27.3 5.3 %collective-permute-start.5 = (f32[32,128]{1,0:T(8,128)S(1)}, f32[32,128]{1,0:T(8,128)S(1)}, u32[]{:S(2)}, u32[]{:S(2)}) collective-permute-start(f32[32,128]{1,0:T(8,128)S(1)} %get-tuple-element.39), channel_id=1, source_target_pairs={{0,127},{1,2},{2,1},{3,4},{4,3},{5,6},{6,5},{7,8},{8,7},{9,10},{10... | collective-permute-start | bytes 49160 | tf_op jit(solution)/shard_map/ppermute | solution.py:45
  27.3 5.3 %collective-permute-start.6 = (f32[32,128]{1,0:T(8,128)S(1)}, f32[32,128]{1,0:T(8,128)S(1)}, u32[]{:S(2)}, u32[]{:S(2)}) collective-permute-start(f32[32,128]{1,0:T(8,128)S(1)} %get-tuple-element.40), channel_id=1, source_target_pairs={{0,2},{1,3},{2,0},{3,1},{4,6},{5,7},{6,4},{7,5},{8,10},{9,11},{10,... | collective-permute-start | bytes 49160 | tf_op jit(solution)/shard_map/ppermute | solution.py:45
  27.3 5.3 %collective-permute-start.7 = (f32[32,128]{1,0:T(8,128)S(1)}, f32[32,128]{1,0:T(8,128)S(1)}, u32[]{:S(2)}, u32[]{:S(2)}) collective-permute-start(f32[32,128]{1,0:T(8,128)S(1)} %get-tuple-element.41), channel_id=1, source_target_pairs={{0,1},{1,0},{2,3},{3,2},{4,5},{5,4},{6,7},{7,6},{8,9},{9,8},{10,11... | collective-permute-start | bytes 49160 | tf_op jit(solution)/shard_map/ppermute | solution.py:45
  33.9 16.9 %collective-permute-start.10 = (f32[7,4,128]{2,1,0:T(4,128)S(1)}, f32[7,4,128]{2,1,0:T(4,128)S(1)}, u32[]{:S(2)}, u32[]{:S(2)}) collective-permute-start(f32[7,4,128]{2,1,0:T(4,128)S(1)} %get-tuple-element.49), channel_id=1, source_target_pairs={{0,1},{1,0},{2,3},{3,2},{4,5},{5,4},{6,7},{7,6},{8,9},{9,8},{10,11... | collective-permute-start | bytes 43016 | tf_op jit(solution)/shard_map/ppermute | solution.py:45
  38.3 12.5 %collective-permute-start.11 = (f32[7,4,128]{2,1,0:T(4,128)S(1)}, f32[7,4,128]{2,1,0:T(4,128)S(1)}, u32[]{:S(2)}, u32[]{:S(2)}) collective-permute-start(f32[7,4,128]{2,1,0:T(4,128)S(1)} %get-tuple-element.50), channel_id=1, source_target_pairs={{0,127},{1,2},{2,1},{3,4},{4,3},{5,6},{6,5},{7,8},{8,7},{9,10},{10... | collective-permute-start | bytes 43016 | tf_op jit(solution)/shard_map/ppermute | solution.py:45
  38.3 12.5 %collective-permute-start.8 = (f32[7,4,128]{2,1,0:T(4,128)S(1)}, f32[7,4,128]{2,1,0:T(4,128)S(1)}, u32[]{:S(2)}, u32[]{:S(2)}) collective-permute-start(f32[7,4,128]{2,1,0:T(4,128)S(1)} %get-tuple-element.47), channel_id=1, source_target_pairs={{0,2},{1,3},{2,0},{3,1},{4,6},{5,7},{6,4},{7,5},{8,10},{9,11},{10,... | collective-permute-start | bytes 43016 | tf_op jit(solution)/shard_map/ppermute | solution.py:45
  38.3 12.5 %collective-permute-start.9 = (f32[7,4,128]{2,1,0:T(4,128)S(1)}, f32[7,4,128]{2,1,0:T(4,128)S(1)}, u32[]{:S(2)}, u32[]{:S(2)}) collective-permute-start(f32[7,4,128]{2,1,0:T(4,128)S(1)} %get-tuple-element.48), channel_id=1, source_target_pairs={{0,126},{1,127},{2,4},{3,5},{4,2},{5,3},{6,8},{7,9},{8,6},{9,7},{1... | collective-permute-start | bytes 43016 | tf_op jit(solution)/shard_map/ppermute | solution.py:45
